TPU v7x, 512 devices: a whole 4x4x16 slice. The times are simulated.
512 devices in a mesh: tm: 64 (over x_lo, z, core), feat: 8 (over x_hi, y).
Axes of the slice: x: 4 (x_hi: 2, x_lo: 2; x = x_hi * 2 + x_lo), y: 4, z: 16, core: 2. Of those that a mesh axis runs over, the one named last changes fastest.
Arguments:
- frames: bfloat16 [32768, 16384], P('tm', 'feat'), may hold values from -24 to 24, as said below
- basis: bfloat16 [16384, 256], P('feat'), may hold values from -6 to 6
Outputs:
- new_basis: float32 [16384, 256], P(('feat', 'tm'))
- reduced: float32 [256, 256], replicated
Inputs may be any that keep to these rules, and one draw needn't show every extreme that they name: `frames`: frames of the trajectory.
All inputs are finite; a program needn't handle non-finite values.
Results may differ from a plain program's by a relative error of at most 0.00365.
Values may be sent and summed in bfloat16 or wider, within the bound.
No kernel may reach another device: no remote copies, remote signals or barrier semaphores. Data moves between devices by JAX's collectives and lax.ppermute only.
A program may use at most 64 MiB of HBM per device.

v0:
```python
import jax
import jax.numpy as jnp
from jax import lax
from jax.sharding import PartitionSpec as P

LAG = 512


def shifted(x, axis, by):
    devices = lax.axis_size(axis)
    pairs = [(i, i + by) for i in range(devices) if 0 <= i + by < devices]
    return lax.ppermute(x, axis, pairs)


def project(block, basis, mean):
    offset_part = jnp.dot(mean, basis.astype(jnp.float32), precision=lax.Precision.HIGHEST)
    summed = lax.psum(jnp.dot(block, basis, preferred_element_type=jnp.float32), "feat")
    offset = lax.psum(offset_part, "feat")
    centred_full = summed - offset[None, :]
    return (centred_full, centred_full.astype(jnp.bfloat16))


def contract(block, weights):
    return lax.dot_general(
        block, weights, (((0,), (0,)), ((), ())), preferred_element_type=jnp.float32
    )


def per_device(frames, basis):
    rows, width = frames.shape
    vecs = basis.shape[1]
    n_time = lax.axis_size("tm")
    total = rows * n_time
    pairs = total - LAG
    first = lax.axis_index("tm") * rows
    frame_ids = first + jnp.arange(rows, dtype=jnp.int32)
    early = (frame_ids < pairs).astype(jnp.bfloat16)
    late = (frame_ids >= LAG).astype(jnp.bfloat16)
    count = early + late
    local_sums = jnp.dot(count[None, :], frames, preferred_element_type=jnp.float32)[0]
    mean = lax.psum(local_sums, "tm") / (2.0 * pairs)
    following = shifted(frames, "tm", -1)
    extended = jnp.concatenate([frames, following], axis=0)
    centred_full, centred_all = project(extended, basis, mean)
    centred_a = centred_all[:rows]
    centred_b = centred_all[LAG : LAG + rows]
    frames_b = extended[LAG : LAG + rows]
    weight_a = jnp.concatenate([early[:, None] * centred_a, early[:, None] * centred_b], axis=1)
    weight_b = jnp.concatenate([early[:, None] * centred_b, early[:, None] * centred_a], axis=1)
    column_sums = jnp.sum(weight_a.astype(jnp.float32), axis=0) + jnp.sum(
        weight_b.astype(jnp.float32), axis=0
    )
    owned = width // n_time
    summed = lax.psum_scatter(
        contract(frames, weight_a)
        + contract(frames_b, weight_b)
        - mean[:, None] * column_sums[None, :],
        "tm",
        scatter_dimension=0,
        tiled=True,
    ) / (2.0 * pairs)
    lagged = summed[:, vecs:]
    own_basis = lax.dynamic_slice_in_dim(basis, lax.axis_index("tm") * owned, owned, 0).astype(
        jnp.float32
    )
    grams = lax.psum(jnp.dot(own_basis.T, summed, precision=lax.Precision.HIGHEST), ("tm", "feat"))
    factor = jnp.linalg.cholesky(grams[:, :vecs])
    new_basis = jax.scipy.linalg.solve_triangular(factor, lagged.T, lower=True).T
    half = jax.scipy.linalg.solve_triangular(factor, grams[:, vecs:], lower=True)
    reduced = jax.scipy.linalg.solve_triangular(factor, half.T, lower=True).T
    return (new_basis, reduced)


def solution(mesh):
    in_specs = (P("tm", "feat"), P("feat", None))
    out_specs = (P(("feat", "tm"), None), P())
    return jax.shard_map(
        per_device, mesh=mesh, in_specs=in_specs, out_specs=out_specs, check_vma=False
    )
```

profile of v0, /device:TPU:6, one launch (start us, length us, event | category | flops | bytes accessed | tf_op | source)
XLA Modules:
  0.0 946.0 jit_solution(11474440042946823345)
XLA Ops:
  7.2 0.0 copy-start
  7.2 0.0 copy-start.1
  7.2 0.0 all-reduce.4.cloned.1.call-start
  7.2 11.4 %collective-permute-start = (bf16[512,2048]{1,0:T(8,128)(2,1)}, bf16[512,2048]{1,0:T(8,128)(2,1)S(1)}, u32[]{:S(2)}, u32[]{:S(2)}) collective-permute-start(bf16[512,2048]{1,0:T(8,128)(2,1)} %param.4), channel_id=1, source_target_pairs={{8,0},{16,8},{24,16},{32,24},{40,32},{48,40},{56,48},{64,56},{72,6... | collective-permute-start | bytes 6291464 | tf_op jit(solution)/shard_map/ppermute | solution.py:12
  18.6 23.8 %collective-permute-done = bf16[512,2048]{1,0:T(8,128)(2,1)S(1)} collective-permute-done((bf16[512,2048]{1,0:T(8,128)(2,1)}, bf16[512,2048]{1,0:T(8,128)(2,1)S(1)}, u32[]{:S(2)}, u32[]{:S(2)}) %collective-permute-start) | collective-permute-done | bytes 2097184 | tf_op jit(solution)/shard_map/ppermute | solution.py:12
  42.5 0.0 copy-start.2
  42.5 1.3 copy-done.2
  43.8 0.0 copy-done
  43.8 3.8 fusion
  47.6 0.0 all-reduce.4.cloned.1.call-update
  47.7 0.0 reduce-scatter.4.cloned.1.call-start
  47.7 0.0 copy-done.1
  47.7 0.4 fusion.33
  48.1 113.2 %psum.29 = f32[2048]{0:T(1024)S(1)} all-reduce(f32[2048]{0:T(1024)S(1)} %bitcast.71), channel_id=1, replica_groups=mesh['tm'=64,'feat'=8] {'tm'}, use_global_device_ids=true, to_apply=%region_1.0 | all-reduce | flops 2048 | bytes 16384 | tf_op jit(solution)/shard_map/psum | solution.py:41
  161.3 0.5 fusion.34
  161.8 22.7 %psum.30 = f32[256]{0:T(256)S(1)} all-reduce(f32[256]{0:T(256)S(1)} %bitcast.72), channel_id=1, replica_groups=mesh['tm'=64,'feat'=8] {'feat'}, use_global_device_ids=true, to_apply=%region_2.0 | all-reduce | flops 256 | bytes 2048 | tf_op jit(solution)/shard_map/psum | solution.py:18
  184.6 0.0 all-reduce.4.cloned.1.call-done
  184.6 1.3 subtract_convert_fusion
  185.9 0.0 copy-start.3
  185.9 0.1 slice_multiply_fusion.1
  186.1 0.2 convert_reduce_fusion
  186.2 1.3 fusion.4
  187.6 0.0 copy-done.3
  187.6 3.5 bitcast_subtract_fusion
  191.1 5.3 copy.11
  196.4 0.0 reduce-scatter.4.cloned.1.call-update
  196.4 0.2 all-reduce.6.cloned.1.call-start
  196.7 219.7 %reduce-scatter.4.cloned.1.call-done = f32[32,512]{1,0:T(8,128)} async-done(((f32[2048,512]{1,0:T(8,128)}), f32[32,512]{1,0:T(8,128)}) %reduce-scatter.4.cloned.1.call-update) | async-done | bytes 65552
  416.3 1.0 copy.12
  417.3 1.2 fusion.21
  418.5 0.0 all-reduce.6.cloned.1.call-update
  418.5 454.4 %all-reduce.6.cloned.1.call-done = f32[256,512]{0,1:T(8,128)} async-done(((f32[256,512]{0,1:T(8,128)}), f32[256,512]{0,1:T(8,128)}) %all-reduce.6.cloned.1.call-update) | async-done | bytes 524304 | tf_op jit(solution)/shard_map/psum | solution.py:66
  873.0 0.0 copy-start.4
  873.0 1.0 slice.105
  874.0 0.1 copy.8
  874.2 1.0 fusion.5
  875.2 11.7 %cholesky.50 = f32[128,128]{1,0:T(8,128)S(1)} custom-call(f32[128,128]{1,0:T(8,128)S(1)} %cholesky.118), custom_call_target="Cholesky" | custom-call | tf_op jit(solution)/shard_map/jit(cholesky)/cholesky | solution.py:67
  887.0 9.8 %custom-call.18 = f32[1,128,128]{1,2,0:T(8,128)S(1)} custom-call(f32[1,128,128]{2,1,0:T(8,128)S(1)} %get-tuple-element.48), custom_call_target="InvertDiagBlocksLowerTriangular" | custom-call | tf_op jit(solution)/shard_map/jit(cholesky)/cholesky | solution.py:67
  896.8 0.2 constant_dynamic-update-slice_fusion.1
  897.0 0.3 convolution_subtract_fusion.3
  897.2 11.7 %cholesky.105 = f32[128,128]{1,0:T(8,128)S(1)} custom-call(f32[128,128]{1,0:T(8,128)S(1)} %convolution_subtract_fusion.3), custom_call_target="Cholesky" | custom-call | tf_op jit(solution)/shard_map/jit(cholesky)/cholesky | solution.py:67
  909.0 0.7 compare_reduce_fusion
  911.1 0.1 triangular_solve.103
  911.2 4.3 while.5
  911.4 0.6 fusion.51
  912.0 1.4 bitcast_dynamic-update-slice_fusion.2
  913.4 0.6 fusion.51
  914.0 1.4 bitcast_dynamic-update-slice_fusion.2
  915.5 19.7 %custom-call.19 = f32[2,128,128]{1,2,0:T(8,128)S(1)} custom-call(f32[2,128,128]{2,1,0:T(8,128)S(1)} %get-tuple-element.18), custom_call_target="InvertDiagBlocksLowerTriangular" | custom-call | tf_op jit(solution)/shard_map/jit(_solve_triangular)/triangular_solve | solution.py:68
  935.1 0.0 copy-done.4
  935.2 0.3 fusion.8
  935.5 0.4 convolution_subtract_fusion.1
  935.9 0.3 fusion.16
  936.2 0.3 fusion.6
  936.5 0.4 convolution_subtract_fusion
  936.9 0.3 fusion.15
  937.3 0.8 copy.9
  938.1 0.3 fusion.10
  938.4 0.2 convolution_subtract_fusion.2
  938.6 0.3 fusion.17
  938.8 0.6 maximum_bitcast_fusion.2
  (18 shorter events, 0.2 us)
Async XLA Ops:
  7.2 36.6 %copy-start = (bf16[2048,256]{1,0:T(8,128)(2,1)S(1)}, bf16[2048,256]{1,0:T(8,128)(2,1)}, u32[]{:S(2)}) copy-start(bf16[2048,256]{1,0:T(8,128)(2,1)} %param.5) | copy-start | bytes 3145732
  7.2 40.6 %copy-start.1 = (bf16[512,2048]{1,0:T(8,128)(2,1)S(1)}, bf16[512,2048]{1,0:T(8,128)(2,1)}, u32[]{:S(2)}) copy-start(bf16[512,2048]{1,0:T(8,128)(2,1)} %param.4) | copy-start | bytes 6291460
  7.2 177.4 %all-reduce.4.cloned.1.call-start = ((), (), s32[]{:S(2)}) async-start(), calls=%async_computation.1 | async-start | bytes 2097152 | tf_op jit(solution)/shard_map/psum | solution.py:17
  7.2 35.2 %collective-permute-start = (bf16[512,2048]{1,0:T(8,128)(2,1)}, bf16[512,2048]{1,0:T(8,128)(2,1)S(1)}, u32[]{:S(2)}, u32[]{:S(2)}) collective-permute-start(bf16[512,2048]{1,0:T(8,128)(2,1)} %param.4), channel_id=1, source_target_pairs={{8,0},{16,8},{24,16},{32,24},{40,32},{48,40},{56,48},{64,56},{72,6... | collective-permute-start | bytes 6291464 | tf_op jit(solution)/shard_map/ppermute | solution.py:12
  42.5 1.4 copy-start.2
  47.7 368.7 %reduce-scatter.4.cloned.1.call-start = ((), (), s32[]{:S(2)}) async-start(), calls=%async_computation.3 | async-start | bytes 4259840
  185.9 1.6 copy-start.3
  196.4 676.6 %all-reduce.6.cloned.1.call-start = ((), (), s32[]{:S(2)}) async-start(), calls=%async_computation.2 | async-start | bytes 1048576 | tf_op jit(solution)/shard_map/psum | solution.py:66
  873.0 62.2 %copy-start.4 = (f32[256,512]{0,1:T(8,128)S(1)}, f32[256,512]{0,1:T(8,128)}, u32[]{:S(2)}) copy-start(f32[256,512]{0,1:T(8,128)} %all-reduce.6.cloned.1.call-done) | copy-start | bytes 1572868
Sparse Core Ops, SparseCore 0:
  47.8 98.0 all-reduce.3
  196.5 219.7 reduce-scatter.3
  422.7 450.2 all-reduce.5
where the time goes:
time: 947 us; the launch traced here: 946 us
  waiting for transfers between devices  698 us (74%)
  blocking collectives  136 us (14%)
  other arithmetic  57.1 us (6%)
  between operations  15.4 us (2%)
  local copies, waits for them, and re-layouts  13.9 us (1%)
  matrix products  13.9 us (1%)
  starting transfers between devices  11.7 us (1%)
    psum x1, waiting for transfers between devices, per_device(): lax.psum(jnp.dot(own_basis.T, summed, precision=lax.Precision.HIGHEST), (...  454 us
    unnamed x4, waiting for transfers between devices  220 us
    psum x1, blocking collectives, per_device(): mean = lax.psum(local_sums, 'tm') / (2.0 * pairs)  113 us
    another operation x6, other arithmetic, per_device(): factor = jnp.linalg.cholesky(grams[:, :vecs])  34 us
    ppermute x1, waiting for transfers between devices, shifted(): return lax.ppermute(x, axis, pairs)  23.8 us
    psum x1, blocking collectives, project(): offset = lax.psum(offset_part, 'feat')  22.7 us
    another operation x3, other arithmetic, per_device(): jax.scipy.linalg.solve_triangular(factor, lagged.T, lower=True)  19.7 us
  transfers between devices with their start and end apart: 4, of which 3 were waited for; matrix products, arithmetic and copies ran while one was open for 0% of the time, Pallas kernels for 0%

commit v1 on v0

v1 whole, which is shorter than its diff:
```python
import jax
import jax.numpy as jnp
from jax import lax
from jax.experimental import pallas as pl
from jax.experimental.pallas import tpu as pltpu
from jax.sharding import Mesh, PartitionSpec as P

TIME = ("xlo", "z", "core")
FEAT = ("xhi", "y")
EXACT = lax.Precision.HIGHEST


def dot(a, b, dims=((1,), (0,)), precision=EXACT):
    return lax.dot_general(
        a, b, (dims, ((), ())), precision=precision, preferred_element_type=jnp.float32
    )


def inverse_factor(block):
    nb = block.shape[0]
    lanes = lax.broadcasted_iota(jnp.int32, (8, nb), 1)
    subs = lax.broadcasted_iota(jnp.int32, (8, nb), 0)
    wide_lanes = lax.broadcasted_iota(jnp.int32, (8, 2 * nb), 1)
    wide_subs = lax.broadcasted_iota(jnp.int32, (8, 2 * nb), 0)
    tiles = [
        jnp.concatenate(
            [block[8 * g : 8 * g + 8], (lanes == subs + 8 * g).astype(jnp.float32)], axis=1
        )
        for g in range(nb // 8)
    ]
    for j in range(nb):
        g, r = divmod(j, 8)
        row = tiles[g][r : r + 1, :]
        hat = row / row[:, j : j + 1]
        for i in range(g, nb // 8):
            column = tiles[i][:, j : j + 1]
            if i == g:
                column = jnp.where(wide_subs[:, :1] > r, column, 0.0)
            tiles[i] = tiles[i] - column * hat
    out = []
    for g in range(nb // 8):
        pivots = jnp.sum(
            jnp.where(wide_lanes == wide_subs + 8 * g, tiles[g], 0.0), axis=1, keepdims=True
        )
        out.append(tiles[g] * lax.rsqrt(pivots))
    return jnp.concatenate(out, axis=0)[:, nb:]


def inverse_cholesky(a, nb):
    n = a.shape[0]
    eye = (
        lax.broadcasted_iota(jnp.int32, (n, n), 0) == lax.broadcasted_iota(jnp.int32, (n, n), 1)
    ).astype(jnp.float32)
    s = jnp.concatenate([a, eye], axis=1)
    rows = []
    for b in range(n // nb):
        t = inverse_factor(s[:nb, nb * b : nb * b + nb])
        p = dot(t, s[:nb])
        rows.append(p[:, n:])
        if nb * (b + 1) < n:
            s = s[nb:] - dot(p[:, nb * (b + 1) : n], p, ((0,), (0,)))
    return jnp.concatenate(rows, axis=0)


def whiten_kernel(blocks, frames_counted, g_ref, inv_ref, reduced_ref, edge_ref, mean_ref):
    n_feat, rows, wide = g_ref.shape
    vecs = n_feat * rows // 2
    part = vecs // n_feat
    half = n_feat // 2
    gram0 = jnp.concatenate([g_ref[k, :, :vecs] for k in range(half)], axis=0)
    gram1 = jnp.concatenate([g_ref[half + k, :, :vecs] for k in range(half)], axis=0)
    u = jnp.concatenate([g_ref[k, :blocks, vecs : vecs + part] for k in range(n_feat)], axis=1)
    z = jnp.concatenate(
        [g_ref[k, :blocks, vecs + part : vecs + 2 * part] for k in range(n_feat)], axis=1
    )
    size = frames_counted / (2.0 * blocks - 2.0)
    ids = lax.broadcasted_iota(jnp.int32, (blocks, 1), 0)
    count = jnp.where((ids == 0) | (ids == blocks - 1), 1.0, 2.0)
    share = count / (2.0 * blocks - 2.0)
    d = u - jnp.sum(share * u, axis=0, keepdims=True)
    y = z + size * d
    nothing = jnp.zeros((1, vecs), jnp.float32)

    def neighbours(x):
        return jnp.concatenate([x[1:], nothing], axis=0) + jnp.concatenate([nothing, x[:-1]], axis=0)

    edge = neighbours(y)
    edge_ref[...] = edge
    mean_ref[...] = jnp.broadcast_to(share, mean_ref.shape)
    across = ((0,), (0,))
    gram0 = (gram0 + dot(d, count * y, across) + dot(z, count * d, across)) / frames_counted
    gram1 = (gram1 + dot(z, neighbours(d), across) + dot(d, edge, across)) / frames_counted
    inv = inverse_cholesky((gram0 + gram0.T) * 0.5, 64)
    inv_ref[...] = inv
    reduced_ref[...] = dot(dot(inv, gram1), inv, ((1,), (1,)))


def finish_kernel(frames_counted, sum_ref, shift_ref, edge_ref, share_ref, inv_ref, out_ref):
    shift = shift_ref[...]
    shift = shift - jnp.sum(share_ref[:, :1] * shift, axis=0, keepdims=True)
    lagged = sum_ref[...] + dot(shift, edge_ref[...], ((0,), (0,)))
    out_ref[...] = dot(lagged / frames_counted, inv_ref[...], ((1,), (1,)))


def call(kernel, out_shape, *args):
    return pl.pallas_call(
        kernel,
        out_shape=out_shape,
        compiler_params=pltpu.CompilerParams(vmem_limit_bytes=40 << 20),
    )(*args)


def swap(x, axis):
    return lax.ppermute(x, axis, [(0, 1), (1, 0)])


def per_device(frames, basis):
    rows, width = frames.shape
    vecs = basis.shape[1]
    n_time, n_feat = lax.axis_size(TIME), lax.axis_size(FEAT)
    n_z = lax.axis_size("z")
    block, part = lax.axis_index(TIME), lax.axis_index(FEAT)
    frames_counted = 2.0 * rows * (n_time - 1)
    count = jnp.where((block == 0) | (block == n_time - 1), 1.0, 2.0)
    f32, bf16 = jnp.float32, jnp.bfloat16

    ones = jnp.ones((1, rows), bf16)
    shift = dot(ones, frames, precision=None)[0] / rows
    projected = dot(frames, basis, precision=None)
    local = jnp.mean(projected, axis=0)
    piece = rows // n_feat
    packed = jnp.concatenate(
        [
            (projected - local).reshape(n_feat, piece, vecs),
            jnp.broadcast_to(local, (n_feat, 8, vecs)),
        ],
        axis=1,
    )
    packed = jnp.sum(lax.all_to_all(packed, FEAT, 0, 0, tiled=True), axis=0)
    centred, offset = packed[:piece].astype(bf16), packed[piece]

    centred = lax.all_to_all(
        jnp.broadcast_to(centred, (n_feat, piece, vecs)), FEAT, 0, 0, tiled=True
    ).reshape(rows, vecs)
    later = lax.ppermute(centred, TIME, [(i + 1, i) for i in range(n_time - 1)])
    earlier = lax.ppermute(centred, TIME, [(i, i + 1) for i in range(n_time - 1)])

    total = jnp.sum(centred.astype(f32), axis=0)
    beside = jnp.sum(later.astype(f32), axis=0) + jnp.sum(earlier.astype(f32), axis=0)

    both = jnp.concatenate([later, earlier], axis=0)
    across = ((0,), (0,))
    lagged = dot(jnp.concatenate([frames, frames], axis=0), both, across, None)
    lagged = lagged - shift[:, None] * beside[None, :]
    owned = width // n_time
    lagged = lagged.reshape(2, n_z, 2, owned, vecs)
    core, xlo = lax.axis_index("core"), lax.axis_index("xlo")
    pick = lax.dynamic_index_in_dim
    lagged = pick(lagged, core, 2, False) + swap(pick(lagged, 1 - core, 2, False), "core")
    lagged = pick(lagged, xlo, 0, False) + swap(pick(lagged, 1 - xlo, 0, False), "xlo")
    lagged = lax.psum_scatter(
        lagged.reshape(n_z * owned, vecs), "z", scatter_dimension=0, tiled=True
    )

    gram_rows = 2 * vecs // n_feat
    first = part % (n_feat // 2) * gram_rows
    left = lax.dynamic_slice_in_dim(centred, first, gram_rows, 1)
    instant = part < n_feat // 2
    right = jnp.concatenate(
        [
            jnp.where(instant, count.astype(bf16) * centred, later),
            jnp.where(instant, jnp.zeros_like(earlier), earlier),
        ],
        axis=0,
    )
    gram = dot(jnp.concatenate([left, left], axis=0), right, across, None)
    each = gram_rows // n_time
    cols = vecs // n_feat
    sums = jnp.concatenate(
        [
            lax.dynamic_slice_in_dim(offset, part * cols, cols, 0),
            lax.dynamic_slice_in_dim(total, part * cols, cols, 0),
        ]
    )
    sent = jnp.concatenate(
        [
            gram.reshape(n_time, each * vecs),
            jnp.broadcast_to(sums, (n_time, 2 * cols)),
            shift.reshape(n_time, owned),
            jnp.zeros((n_time, -(2 * cols + owned) % 128), f32),
        ],
        axis=1,
    )
    got = lax.all_to_all(sent, TIME, 0, 0, tiled=True)
    gram = jnp.sum(got[:, : each * vecs], axis=0)
    sums = got[:, each * vecs : each * vecs + 2 * cols]
    shifts = got[:, each * vecs + 2 * cols : each * vecs + 2 * cols + owned]
    gram = lax.all_to_all(
        jnp.broadcast_to(gram, (n_time, each * vecs)), TIME, 0, 0, tiled=True
    ).reshape(gram_rows, vecs)
    sums = jnp.pad(sums, ((0, gram_rows - n_time), (0, -2 * cols % 128)))
    slices = jnp.concatenate([gram, sums], axis=1)
    slices = lax.all_to_all(
        jnp.broadcast_to(slices, (n_feat,) + slices.shape), FEAT, 0, 0, tiled=True
    )

    square = jax.ShapeDtypeStruct((vecs, vecs), f32)
    inv, reduced, edge, share = call(
        lambda *refs: whiten_kernel(n_time, frames_counted, *refs),
        [
            square,
            square,
            jax.ShapeDtypeStruct((n_time, vecs), f32),
            jax.ShapeDtypeStruct((n_time, 128), f32),
        ],
        slices,
    )
    new_basis = call(
        lambda *refs: finish_kernel(frames_counted, *refs),
        jax.ShapeDtypeStruct((owned, vecs), f32),
        lagged,
        shifts,
        edge,
        share,
        inv,
    )
    return (new_basis, reduced)


def solution(mesh):
    n_time, n_feat = mesh.devices.shape
    mesh = Mesh(mesh.devices.reshape(2, n_time // 4, 2, 2, n_feat // 2), TIME + FEAT)
    return jax.shard_map(
        per_device,
        mesh=mesh,
        in_specs=(P(TIME, FEAT), P(FEAT, None)),
        out_specs=(P(FEAT + TIME, None), P()),
        check_vma=False,
    )
```

time: 947 us -> 185 us (0.20)
  waiting for transfers between devices: 698 us -> 53.7 us
  blocking collectives: 136 us -> 28 us
  other arithmetic: 57.1 us -> 5.5 us
  starting transfers between devices: 11.7 us -> 42 us
  Pallas kernels: 0 us -> 28.1 us
    psum x2 -> x0, waiting for transfers between devices: 454 us -> none  [the longest x1 454 us: per_device(): lax.psum(jnp.dot(own_basis.T, summed, precision=lax.Precision.HIGHEST), (...]
    unnamed x4 -> x1, waiting for transfers between devices: 220 us -> 0.02 us
    psum x2 -> x0, blocking collectives: 136 us -> none  [the longest x1 113 us: per_device(): mean = lax.psum(local_sums, 'tm') / (2.0 * pairs)]
    another operation x9 -> x0, other arithmetic: 53.7 us -> none  [the longest x6 34 us: per_device(): factor = jnp.linalg.cholesky(grams[:, :vecs])]
    all_to_all x0 -> x3, waiting for transfers between devices: none -> 38.8 us  [the longest x1 14.5 us: per_device(): got = lax.all_to_all(sent, TIME, 0, 0, tiled=True)]
    pallas_call x0 -> x2, Pallas kernels: none -> 28.1 us  [call(): pl.pallas_call(kernel, out_shape=out_shape, compiler_params=pltpu.Compile...]
    all_to_all x0 -> x2, blocking collectives: none -> 28 us  [the longest x1 16.7 us: per_device(): packed = jnp.sum(lax.all_to_all(packed, FEAT, 0, 0, tiled=True), axis=0)]
    all_to_all x0 -> x3, starting transfers between devices: none -> 27.2 us  [the longest x1 14.8 us: per_device(): got = lax.all_to_all(sent, TIME, 0, 0, tiled=True)]
  transfers between devices with their start and end apart: 4 -> 8, of which waited for: 3 -> 6; matrix products, arithmetic and copies ran while one was open for 0% -> 5% of each run, Pallas kernels for 0% -> 15%
where the time goes in v1:
time: 185 us; the launch traced here: 184 us
  waiting for transfers between devices  53.7 us (29%)
  starting transfers between devices  42 us (23%)
  Pallas kernels  28.1 us (15%)
  blocking collectives  28 us (15%)
  between operations  14.3 us (8%)
  matrix products  7.06 us (4%)
  other arithmetic  5.5 us (3%)
  local copies, waits for them, and re-layouts  5.01 us (3%)
    pallas_call x2, Pallas kernels, call(): pl.pallas_call(kernel, out_shape=out_shape, compiler_params=pltpu.Compile...  28.1 us
    all_to_all x1, blocking collectives, per_device(): packed = jnp.sum(lax.all_to_all(packed, FEAT, 0, 0, tiled=True), axis=0)  16.7 us
    all_to_all x1, starting transfers between devices, per_device(): got = lax.all_to_all(sent, TIME, 0, 0, tiled=True)  14.8 us
    all_to_all x1, waiting for transfers between devices, per_device(): got = lax.all_to_all(sent, TIME, 0, 0, tiled=True)  14.5 us
    all_to_all x1, waiting for transfers between devices, per_device(): lax.all_to_all(jnp.broadcast_to(gram, (n_time, each * vecs)), TIME, 0, 0,...  12.3 us
    reduce_scatter x1, waiting for transfers between devices, per_device(): lax.psum_scatter(lagged.reshape(n_z * owned, vecs), 'z', scatter_dimensio...  12.3 us
    all_to_all x1, waiting for transfers between devices, per_device(): lax.all_to_all(jnp.broadcast_to(slices, (n_feat,) + slices.shape), FEAT,...  11.9 us
    all_to_all x1, blocking collectives, per_device(): lax.all_to_all(jnp.broadcast_to(centred, (n_feat, piece, vecs)), FEAT, 0,...  11.3 us
  transfers between devices with their start and end apart: 8, of which 6 were waited for; matrix products, arithmetic and copies ran while one was open for 5% of the time, Pallas kernels for 15%

profile of v1, /device:TPU:6, one launch (start us, length us, event | category | flops | bytes accessed | tf_op | source)
XLA Modules:
  0.0 183.7 jit_solution(6462774743115426821)
XLA Ops:
  7.2 0.0 copy-start
  7.2 1.2 copy-done
  8.4 2.3 %fusion.23 = (f32[256]{0:T(256)S(1)}, f32[512,256]{1,0:T(8,128)S(1)}) fusion(bf16[512,2048]{1,0:T(8,128)(2,1)} %param.2, bf16[2048,256]{1,0:T(8,128)(2,1)S(1)} %copy-done), kind=kOutput, calls=%fused_computation.44 | convolution fusion | flops 537001728 | bytes 3671040 | tf_op jit(solution)/shard_map/dot_general | solution.py:14
  10.8 16.7 %all_to_all.36 = f32[8,72,256]{2,1,0:T(8,128)S(1)} all-to-all(f32[8,72,256]{2,1,0:T(8,128)S(1)} %pad_maximum_fusion), channel_id=1, replica_groups=mesh['xlo'=2,'z'=16,'core'=2,'xhi'=2,'y'=4] {'xhi','y'}, dimensions={0} | all-to-all | bytes 1179648 | tf_op jit(solution)/shard_map/all_to_all | solution.py:139
  27.6 0.0 copy-start.3
  27.6 0.0 copy-start.2
  27.6 11.3 %all_to_all.37 = bf16[8,64,256]{2,1,0:T(8,128)(2,1)S(1)} all-to-all(bf16[8,64,256]{2,1,0:T(8,128)(2,1)S(1)} %broadcast_in_dim.26), channel_id=1, replica_groups=mesh['xlo'=2,'z'=16,'core'=2,'xhi'=2,'y'=4] {'xhi','y'}, dimensions={0} | all-to-all | bytes 524288 | tf_op jit(solution)/shard_map/all_to_all | solution.py:142
  39.0 1.9 %collective-permute-start.1 = (bf16[512,256]{1,0:T(8,128)(2,1)S(1)}, bf16[512,256]{1,0:T(8,128)(2,1)}, u32[]{:S(2)}, u32[]{:S(2)}) collective-permute-start(bf16[512,256]{1,0:T(8,128)(2,1)S(1)} %bitcast.27), channel_id=1, source_target_pairs={{0,8},{8,16},{16,24},{24,32},{32,40},{40,48},{48,56},{56,64},{64,7... | collective-permute-start | bytes 786440 | tf_op jit(solution)/shard_map/ppermute | solution.py:146
  40.9 2.0 %fusion.17 = f32[1,2048]{1,0:T(1,128)S(1)} fusion(bf16[512,2048]{1,0:T(8,128)(2,1)} %param.2), kind=kOutput, calls=%fused_computation.37 | convolution fusion | flops 2097152 | bytes 2105344 | tf_op jit(solution)/shard_map/dot_general | solution.py:14
  42.8 9.0 %collective-permute-start = (bf16[512,256]{1,0:T(8,128)(2,1)S(1)}, bf16[512,256]{1,0:T(8,128)(2,1)}, u32[]{:S(2)}, u32[]{:S(2)}) collective-permute-start(bf16[512,256]{1,0:T(8,128)(2,1)S(1)} %bitcast.28), channel_id=1, source_target_pairs={{8,0},{16,8},{24,16},{32,24},{40,32},{48,40},{56,48},{64,56},{72,6... | collective-permute-start | bytes 786440 | tf_op jit(solution)/shard_map/ppermute | solution.py:145
  51.9 0.1 reshape.42
  52.0 0.1 pad.10.clone
  52.0 0.1 collective-permute-done.1
  52.1 1.0 convert_reduce_fusion.1
  53.2 2.6 %collective-permute-done = bf16[512,256]{1,0:T(8,128)(2,1)} collective-permute-done((bf16[512,256]{1,0:T(8,128)(2,1)S(1)}, bf16[512,256]{1,0:T(8,128)(2,1)}, u32[]{:S(2)}, u32[]{:S(2)}) %collective-permute-start) | collective-permute-done | bytes 262176 | tf_op jit(solution)/shard_map/ppermute | solution.py:145
  55.7 1.0 convert_reduce_fusion.2
  56.8 0.0 copy-done.2
  56.8 2.5 %fusion.4 = f32[2048,256]{1,0:T(8,128)S(1)} fusion(bf16[512,2048]{1,0:T(8,128)(2,1)S(1)} %copy-done.2, f32[256]{0:T(256)S(1)} %add.53, f32[2048]{0:T(1024)S(1)} %broadcast_multiply_fusion, bf16[512,256]{1,0:T(8,128)(2,1)} %collective-permute-done.1, bf16[512,256]{1,0:T(8,128)(2,1)} %collective-permute-done), kind=kOutput, calls=%fused_computation.4 | convolution fusion | flops 1084227584 | bytes 4727808 | tf_op jit(solution)/shard_map/dot_general | solution.py:14
  59.3 0.0 copy-done.3
  59.3 0.0 slice-start
  59.3 0.1 dynamic-slice_bitcast_fusion
  59.4 1.9 %collective-permute-start.2 = (f32[2,16,32,256]{3,2,1,0:T(8,128)S(1)}, f32[2,16,32,256]{3,2,1,0:T(8,128)S(1)}, u32[]{:S(2)}, u32[]{:S(2)}) collective-permute-start(f32[2,16,32,256]{3,2,1,0:T(8,128)S(1)} %dynamic-slice_bitcast_fusion), channel_id=1, source_target_pairs={{0,8},{8,0},{1,9},{9,1},{2,10},{10,2},{3,11},{11,3},{4,12},{12,4},... | collective-permute-start | bytes 3145736 | tf_op jit(solution)/shard_map/ppermute | solution.py:114
  61.4 0.0 slice-done
  61.4 0.1 fusion.19
  61.4 0.1 convert_reduce_fusion
  61.5 0.1 dynamic_slice.32
  61.6 0.1 pad_maximum_fusion.1
  61.7 0.1 constant_dynamic-slice_fusion.1
  61.8 1.0 broadcast_select_fusion
  62.8 1.0 multiply_select_fusion
  63.8 0.2 fusion.10
  64.0 0.0 collective-permute-done.2
  64.0 0.2 bitcast_add_fusion
  64.3 1.9 %collective-permute-start.3 = (f32[16,32,256]{2,1,0:T(8,128)S(1)}, f32[16,32,256]{2,1,0:T(8,128)S(1)}, u32[]{:S(2)}, u32[]{:S(2)}) collective-permute-start(f32[16,32,256]{2,1,0:T(8,128)S(1)} %dynamic-slice_bitcast_fusion.1), channel_id=1, source_target_pairs={{0,256},{256,0},{1,257},{257,1},{2,258},{258,2},{3,259},{259,3},{4... | collective-permute-start | bytes 1572872 | tf_op jit(solution)/shard_map/ppermute | solution.py:114
  66.2 0.1 maximum_bitcast_fusion
  66.3 0.7 copy.5
  67.0 14.8 %all-to-all-start.2 = ((f32[64,1,384]{2,1,0:T(1,128)}), f32[64,1,384]{2,1,0:T(1,128)S(1)}, u32[]{:S(2)}, u32[]{:S(2)}) async-start(f32[64,1,384]{2,1,0:T(1,128)} %copy.5), calls=%async_computation.3 | async-start | bytes 196608 | tf_op jit(solution)/shard_map/all_to_all | solution.py:194
  81.8 14.5 %all-to-all-done.2 = f32[64,1,384]{2,1,0:T(1,128)S(1)} async-done(((f32[64,1,384]{2,1,0:T(1,128)}), f32[64,1,384]{2,1,0:T(1,128)S(1)}, u32[]{:S(2)}, u32[]{:S(2)}) %all-to-all-start.2) | async-done | bytes 98336 | tf_op jit(solution)/shard_map/all_to_all | solution.py:194
  96.4 0.7 broadcast_in_dim.30
  97.0 5.9 %all-to-all-start.3 = ((f32[64,1,256]{2,1,0:T(1,128)}), f32[64,1,256]{2,1,0:T(1,128)S(1)}, u32[]{:S(2)}, u32[]{:S(2)}) async-start(f32[64,1,256]{2,1,0:T(1,128)} %broadcast_in_dim.30), calls=%async_computation.4 | async-start | bytes 131072 | tf_op jit(solution)/shard_map/all_to_all | solution.py:198
  102.9 0.0 reduce-scatter.2.cloned.1.call-start
  103.0 0.0 collective-permute-done.3
  103.0 0.9 bitcast_add_fusion.1
  103.9 0.0 reduce-scatter.2.cloned.1.call-update
  103.9 12.3 %all-to-all-done.3 = f32[64,1,256]{2,1,0:T(1,128)S(1)} async-done(((f32[64,1,256]{2,1,0:T(1,128)}), f32[64,1,256]{2,1,0:T(1,128)S(1)}, u32[]{:S(2)}, u32[]{:S(2)}) %all-to-all-start.3) | async-done | bytes 65568 | tf_op jit(solution)/shard_map/all_to_all | solution.py:198
  116.2 0.9 broadcast_in_dim.31
  117.2 6.6 %all-to-all-start.4 = ((f32[8,64,384]{2,1,0:T(8,128)}), f32[8,64,384]{2,1,0:T(8,128)S(1)}, u32[]{:S(2)}, u32[]{:S(2)}) async-start(f32[8,64,384]{2,1,0:T(8,128)} %broadcast_in_dim.31), calls=%async_computation.5 | async-start | bytes 1572864 | tf_op jit(solution)/shard_map/all_to_all | solution.py:203
  123.7 0.1 slice.23.refs_1_
  123.8 11.9 %all-to-all-done.4.refs_0_ = f32[8,64,384]{2,1,0:T(8,128)S(1)} async-done(((f32[8,64,384]{2,1,0:T(8,128)}), f32[8,64,384]{2,1,0:T(8,128)S(1)}, u32[]{:S(2)}, u32[]{:S(2)}) %all-to-all-start.4) | async-done | bytes 786464 | tf_op jit(solution)/shard_map/all_to_all | solution.py:203
  135.8 26.9 %shard_map.41 = (f32[256,256]{1,0:T(8,128)S(1)}, f32[256,256]{1,0:T(8,128)}, f32[64,256]{1,0:T(8,128)S(1)}, f32[64,128]{1,0:T(8,128)S(1)}) custom-call(f32[8,64,384]{2,1,0:T(8,128)S(1)} %all-to-all-done.4.refs_0_), custom_call_target="tpu_custom_call" | custom-call | tf_op jit(solution)/shard_map/pallas_call | solution.py:106
  162.7 12.3 %reduce-scatter.2.cloned.1.call-done.refs_0_ = f32[32,256]{1,0:T(8,128)} async-done(((f32[512,256]{1,0:T(8,128)}), f32[32,256]{1,0:T(8,128)}) %reduce-scatter.2.cloned.1.call-update) | async-done | bytes 32784 | tf_op jit(solution)/shard_map/reduce_scatter | solution.py:161
  174.9 0.0 copy-start.1
  174.9 0.8 copy-done.1
  175.7 1.2 shard_map.42
  (16 shorter events, 0.3 us)
Async XLA Ops:
  7.2 1.2 copy-start
  27.6 31.8 %copy-start.3 = (f32[72,256]{1,0:T(8,128)}, f32[72,256]{1,0:T(8,128)S(1)}, u32[]{:S(2)}) copy-start(f32[72,256]{1,0:T(8,128)S(1)} %reduce_sum.55) | copy-start | bytes 221188
  27.6 29.2 %copy-start.2 = (bf16[512,2048]{1,0:T(8,128)(2,1)S(1)}, bf16[512,2048]{1,0:T(8,128)(2,1)}, u32[]{:S(2)}) copy-start(bf16[512,2048]{1,0:T(8,128)(2,1)} %param.2) | copy-start | bytes 6291460
  39.0 13.2 %collective-permute-start.1 = (bf16[512,256]{1,0:T(8,128)(2,1)S(1)}, bf16[512,256]{1,0:T(8,128)(2,1)}, u32[]{:S(2)}, u32[]{:S(2)}) collective-permute-start(bf16[512,256]{1,0:T(8,128)(2,1)S(1)} %bitcast.27), channel_id=1, source_target_pairs={{0,8},{8,16},{16,24},{24,32},{32,40},{40,48},{48,56},{56,64},{64,7... | collective-permute-start | bytes 786440 | tf_op jit(solution)/shard_map/ppermute | solution.py:146
  42.8 12.9 %collective-permute-start = (bf16[512,256]{1,0:T(8,128)(2,1)S(1)}, bf16[512,256]{1,0:T(8,128)(2,1)}, u32[]{:S(2)}, u32[]{:S(2)}) collective-permute-start(bf16[512,256]{1,0:T(8,128)(2,1)S(1)} %bitcast.28), channel_id=1, source_target_pairs={{8,0},{16,8},{24,16},{32,24},{40,32},{48,40},{56,48},{64,56},{72,6... | collective-permute-start | bytes 786440 | tf_op jit(solution)/shard_map/ppermute | solution.py:145
  59.3 2.0 %slice-start = ((f32[72,256]{1,0:T(8,128)}), f32[1,256]{1,0:T(1,128)S(1)}, s32[]{:S(2)}) async-start(f32[72,256]{1,0:T(8,128)} %copy-done.3), calls=%async_computation.7 | async-start | bytes 2048 | tf_op jit(solution)/shard_map/slice | solution.py:140
  59.4 4.6 %collective-permute-start.2 = (f32[2,16,32,256]{3,2,1,0:T(8,128)S(1)}, f32[2,16,32,256]{3,2,1,0:T(8,128)S(1)}, u32[]{:S(2)}, u32[]{:S(2)}) collective-permute-start(f32[2,16,32,256]{3,2,1,0:T(8,128)S(1)} %dynamic-slice_bitcast_fusion), channel_id=1, source_target_pairs={{0,8},{8,0},{1,9},{9,1},{2,10},{10,2},{3,11},{11,3},{4,12},{12,4},... | collective-permute-start | bytes 3145736 | tf_op jit(solution)/shard_map/ppermute | solution.py:114
  64.3 38.7 %collective-permute-start.3 = (f32[16,32,256]{2,1,0:T(8,128)S(1)}, f32[16,32,256]{2,1,0:T(8,128)S(1)}, u32[]{:S(2)}, u32[]{:S(2)}) collective-permute-start(f32[16,32,256]{2,1,0:T(8,128)S(1)} %dynamic-slice_bitcast_fusion.1), channel_id=1, source_target_pairs={{0,256},{256,0},{1,257},{257,1},{2,258},{258,2},{3,259},{259,3},{4... | collective-permute-start | bytes 1572872 | tf_op jit(solution)/shard_map/ppermute | solution.py:114
  67.0 29.3 %all-to-all-start.2 = ((f32[64,1,384]{2,1,0:T(1,128)}), f32[64,1,384]{2,1,0:T(1,128)S(1)}, u32[]{:S(2)}, u32[]{:S(2)}) async-start(f32[64,1,384]{2,1,0:T(1,128)} %copy.5), calls=%async_computation.3 | async-start | bytes 196608 | tf_op jit(solution)/shard_map/all_to_all | solution.py:194
  97.0 19.2 %all-to-all-start.3 = ((f32[64,1,256]{2,1,0:T(1,128)}), f32[64,1,256]{2,1,0:T(1,128)S(1)}, u32[]{:S(2)}, u32[]{:S(2)}) async-start(f32[64,1,256]{2,1,0:T(1,128)} %broadcast_in_dim.30), calls=%async_computation.4 | async-start | bytes 131072 | tf_op jit(solution)/shard_map/all_to_all | solution.py:198
  102.9 72.0 %reduce-scatter.2.cloned.1.call-start = ((), (), s32[]{:S(2)}) async-start(), calls=%async_computation.6 | async-start | bytes 557056 | tf_op jit(solution)/shard_map/reduce_scatter | solution.py:161
  117.2 18.6 %all-to-all-start.4 = ((f32[8,64,384]{2,1,0:T(8,128)}), f32[8,64,384]{2,1,0:T(8,128)S(1)}, u32[]{:S(2)}, u32[]{:S(2)}) async-start(f32[8,64,384]{2,1,0:T(8,128)} %broadcast_in_dim.31), calls=%async_computation.5 | async-start | bytes 1572864 | tf_op jit(solution)/shard_map/all_to_all | solution.py:203
  174.9 0.8 copy-start.1
Sparse Core Ops, SparseCore 0:
  106.5 68.3 reduce-scatter.1

commit v2 on v1

v2 whole, which is shorter than its diff:
```python
import jax
import jax.numpy as jnp
from jax import lax
from jax.experimental import pallas as pl
from jax.experimental.pallas import tpu as pltpu
from jax.sharding import Mesh, PartitionSpec as P

TIME = ("xlo", "z", "core")
FEAT = ("xhi", "y")
EXACT = lax.Precision.HIGHEST


def dot(a, b, dims=((1,), (0,)), precision=EXACT):
    return lax.dot_general(
        a, b, (dims, ((), ())), precision=precision, preferred_element_type=jnp.float32
    )


def inverse_factor(block):
    nb = block.shape[0]
    wide, count = 2 * nb, nb // 8
    lanes = lax.broadcasted_iota(jnp.int32, (8, nb), 1)
    subs = lax.broadcasted_iota(jnp.int32, (8, nb), 0)
    below = lax.broadcasted_iota(jnp.int32, (8, wide), 0)
    tiles = [
        jnp.concatenate(
            [block[8 * g : 8 * g + 8], (lanes == subs + 8 * g).astype(jnp.float32)], axis=1
        )
        for g in range(count)
    ]
    out = []
    for g in range(count):
        spread = [
            [jnp.broadcast_to(tiles[i][:, 8 * g + k : 8 * g + k + 1], (8, wide)) for i in range(g, count)]
            for k in range(8)
        ]
        rows = tiles[g]
        for r in range(0, 8, 2):
            c0, c1 = spread[r], spread[r + 1]
            p, q, s = c0[0][r : r + 1], c1[0][r : r + 1], c1[0][r + 1 : r + 2]
            det = p * s - q * q
            inv = 1.0 / det
            pi, qi, si = p * inv, q * inv, s * inv
            for k in range(r + 2, 8):
                x, y = spread[k][0][r : r + 1], spread[k][0][r + 1 : r + 2]
                gx, gy = si * x - qi * y, pi * y - qi * x
                for i in range(count - g):
                    spread[k][i] = spread[k][i] - (c0[i] * gx + c1[i] * gy)
            a, b = rows[r : r + 1], rows[r + 1 : r + 2]
            v = p * b - q * a
            ga, gb = si * a - qi * b, v * inv
            out.append(a * lax.rsqrt(p))
            out.append(v * lax.rsqrt(p * det))
            if r < 6:
                keep = below > r + 1
                rows = rows - (jnp.where(keep, c0[0], 0.0) * ga + jnp.where(keep, c1[0], 0.0) * gb)
            for i in range(g + 1, count):
                tiles[i] = tiles[i] - (c0[i - g] * ga + c1[i - g] * gb)
    return jnp.concatenate(out, axis=0)[:, nb:]


def inverse_cholesky(a, nb):
    n = a.shape[0]
    eye = lax.broadcasted_iota(jnp.int32, (n, n), 0) == lax.broadcasted_iota(jnp.int32, (n, n), 1)
    diagonal = jnp.where(eye, a, 0.0)
    down = lax.rsqrt(jnp.sum(diagonal, axis=1, keepdims=True))
    along = lax.rsqrt(jnp.sum(diagonal, axis=0, keepdims=True))
    s = jnp.concatenate([a * down * along, eye.astype(jnp.float32)], axis=1)
    rows = []
    for b in range(n // nb):
        t = inverse_factor(s[:nb, nb * b : nb * b + nb])
        p = dot(t, s[:nb])
        rows.append(p[:, n:])
        if nb * (b + 1) < n:
            s = s[nb:] - dot(p[:, nb * (b + 1) : n], p, ((0,), (0,)))
    return jnp.concatenate(rows, axis=0) * along


def whiten_kernel(blocks, frames_counted, g_ref, inv_ref, reduced_ref, edge_ref, mean_ref):
    n_feat, rows, wide = g_ref.shape
    vecs = n_feat * rows // 2
    part = vecs // n_feat
    half = n_feat // 2
    gram0 = jnp.concatenate([g_ref[k, :, :vecs] for k in range(half)], axis=0)
    gram1 = jnp.concatenate([g_ref[half + k, :, :vecs] for k in range(half)], axis=0)
    u = jnp.concatenate([g_ref[k, :blocks, vecs : vecs + part] for k in range(n_feat)], axis=1)
    z = jnp.concatenate(
        [g_ref[k, :blocks, vecs + part : vecs + 2 * part] for k in range(n_feat)], axis=1
    )
    size = frames_counted / (2.0 * blocks - 2.0)
    ids = lax.broadcasted_iota(jnp.int32, (blocks, 1), 0)
    count = jnp.where((ids == 0) | (ids == blocks - 1), 1.0, 2.0)
    share = count / (2.0 * blocks - 2.0)
    d = u - jnp.sum(share * u, axis=0, keepdims=True)
    y = z + size * d
    nothing = jnp.zeros((1, vecs), jnp.float32)

    def neighbours(x):
        return jnp.concatenate([x[1:], nothing], axis=0) + jnp.concatenate([nothing, x[:-1]], axis=0)

    edge = neighbours(y)
    edge_ref[...] = edge
    mean_ref[...] = jnp.broadcast_to(share, mean_ref.shape)
    across = ((0,), (0,))
    gram0 = (gram0 + dot(d, count * y, across) + dot(z, count * d, across)) / frames_counted
    gram1 = (gram1 + dot(z, neighbours(d), across) + dot(d, edge, across)) / frames_counted
    inv = inverse_cholesky((gram0 + gram0.T) * 0.5, 64)
    inv_ref[...] = inv
    reduced_ref[...] = dot(dot(inv, gram1), inv, ((1,), (1,)))


def finish_kernel(frames_counted, sum_ref, shift_ref, edge_ref, share_ref, inv_ref, out_ref):
    shift = shift_ref[...]
    shift = shift - jnp.sum(share_ref[:, :1] * shift, axis=0, keepdims=True)
    lagged = jnp.sum(sum_ref[...].astype(jnp.float32), axis=0) + dot(shift, edge_ref[...], ((0,), (0,)))
    out_ref[...] = dot(lagged / frames_counted, inv_ref[...], ((1,), (1,)))


def project_kernel(frames_ref, basis_ref, packed_ref):
    step, steps = pl.program_id(0), pl.num_programs(0)
    pieces, tall, vecs = packed_ref.shape
    piece = tall - 8
    each = pieces // steps
    block = dot(frames_ref[...], basis_ref[...], precision=None)
    packed_ref[pl.ds(step * each, each), :piece] = block.reshape(each, piece, vecs)

    @pl.when(step == steps - 1)
    def _():
        values = packed_ref[:, :piece]
        local = jnp.sum(jnp.sum(values, axis=0), axis=0, keepdims=True) / (pieces * piece)
        packed_ref[:, :piece] = values - local[None]
        packed_ref[:, piece:] = jnp.broadcast_to(local[None], (pieces, 8, vecs))


def shift_kernel(frames_ref, out_ref):
    n_time, lanes = out_ref.shape
    rows, width = frames_ref.shape
    owned = width // n_time
    step = width // 4
    hit = lax.broadcasted_iota(jnp.int32, (owned, lanes), 0) == lax.broadcasted_iota(
        jnp.int32, (owned, lanes), 1
    )
    ones = jnp.ones((rows, lanes), jnp.bfloat16)
    for i in range(4):
        sums = dot(frames_ref[:, i * step : (i + 1) * step], ones, ((0,), (0,)), None)
        sums = jnp.where(hit[None], sums.reshape(step // owned, owned, lanes), 0.0)
        rows_here = n_time // 4
        out_ref[i * rows_here : (i + 1) * rows_here] = jnp.sum(sums, axis=1) / rows


def collect_kernel(got_ref, centred_ref, offset_ref):
    piece = centred_ref.shape[1]
    total = jnp.sum(got_ref[...], axis=0)
    offset_ref[...] = total[piece:]
    centred_ref[...] = jnp.broadcast_to(total[:piece].astype(jnp.bfloat16)[None], centred_ref.shape)


def gram_kernel(
    place_ref, centred_ref, first_ref, second_ref, offset_ref, shift_ref, sent_ref, beside_ref, gram_ref
):
    n_time, each, wide = sent_ref.shape
    vecs = gram_ref.shape[0]
    part, n_feat, count = place_ref[0], place_ref[1], place_ref[2]
    half = n_feat // 2
    across = ((0,), (0,))
    first, second = first_ref[...], second_ref[...]
    beside = jnp.sum(first.astype(jnp.float32), axis=0, keepdims=True) + jnp.sum(
        second.astype(jnp.float32), axis=0, keepdims=True
    )
    beside_ref[...] = jnp.broadcast_to(beside, beside_ref.shape)

    @pl.when(part < half)
    def _():
        gram_ref[...] = count.astype(jnp.float32) * dot(
            centred_ref[...], centred_ref[...], across, None
        )

    @pl.when(part >= half)
    def _():
        gram_ref[...] = dot(centred_ref[...], first, across, None) + dot(
            centred_ref[...], second, across, None
        )

    rows = n_time * each
    mine = gram_ref[pl.ds(pl.multiple_of(lax.rem(part, half) * rows, rows), rows), :]
    part_cols = rows // 2
    total = jnp.sum(centred_ref[...].astype(jnp.float32), axis=0, keepdims=True)
    both = jnp.concatenate(
        [offset_ref[:4], jnp.broadcast_to(total, (4, vecs))], axis=0
    )
    both = pltpu.roll(both, lax.rem(n_feat - part, n_feat) * part_cols, 1)[:, :part_cols]
    extra = jnp.concatenate(
        [
            jnp.broadcast_to(both[:1], (n_time, part_cols)),
            jnp.broadcast_to(both[4:5], (n_time, part_cols)),
            shift_ref[:, : wide - vecs - 2 * part_cols],
        ],
        axis=1,
    )
    for i in range(n_time):
        sent_ref[i, :, :vecs] = mine[i * each : (i + 1) * each]
        sent_ref[i, :, vecs:] = jnp.broadcast_to(extra[i : i + 1], (each, wide - vecs))


def total_kernel(got_ref, row_ref, sums_ref, shift_ref):
    n_time, each, vecs = row_ref.shape
    total = got_ref[0, :, :vecs]
    for i in range(1, n_time):
        total = total + got_ref[i, :, :vecs]
    low = vecs + sums_ref.shape[1]
    for i in range(n_time):
        row_ref[i] = total
        sums_ref[i : i + 1] = got_ref[i, :1, vecs:low]
        shift_ref[i : i + 1] = got_ref[i, :1, low : low + shift_ref.shape[1]]


def slices_kernel(rows_ref, sums_ref, out_ref):
    n_feat, height, wide = out_ref.shape
    n_time, each, vecs = rows_ref.shape
    for i in range(n_time):
        out_ref[0, i * each : (i + 1) * each, :vecs] = rows_ref[i]
    side = jnp.zeros((n_time, wide - vecs - sums_ref.shape[1]), jnp.float32)
    out_ref[0, :n_time, vecs:] = jnp.concatenate([sums_ref[...], side], axis=1)
    if height > n_time:
        out_ref[0, n_time:, vecs:] = jnp.zeros((height - n_time, wide - vecs), jnp.float32)
    for k in range(1, n_feat):
        out_ref[k] = out_ref[0]


def contract_kernel(core_ref, frames_ref, first_ref, second_ref, beside_ref, kept_ref, given_ref, all_ref):
    owned = kept_ref.shape[1]
    rows, width = frames_ref.shape
    step = 8 * owned
    across = ((0,), (0,))
    beside = beside_ref[:1] / rows
    ones = jnp.ones((rows, 128), jnp.bfloat16)
    for i in range(width // step):
        frames = frames_ref[:, i * step : (i + 1) * step]
        sums = dot(frames, first_ref[...], across, None) + dot(frames, second_ref[...], across, None)
        total = dot(frames, ones, across, None)
        total = jnp.concatenate([total] * (sums.shape[1] // 128), axis=1)
        sums = sums - total * beside
        all_ref[4 * i : 4 * i + 4] = sums.reshape(4, 2, owned, sums.shape[1])
    core = core_ref[0]
    kept_ref[...] = all_ref[:, core]
    given_ref[...] = all_ref[:, 1 - core]


def halve_kernel(xlo_ref, kept_ref, got_ref, mine_ref, given_ref):
    xlo = xlo_ref[0]
    half = mine_ref.shape[0]
    own, other = pl.ds(xlo * half, half), pl.ds((1 - xlo) * half, half)
    mine_ref[...] = kept_ref[own] + got_ref[own]
    given_ref[...] = kept_ref[other] + got_ref[other]


def call(kernel, out_shape, *args, scalars=0, scratch=(), flops=0):
    vmem = pl.BlockSpec(memory_space=pltpu.VMEM)
    scalar = pl.BlockSpec(memory_space=pltpu.SMEM)
    return pl.pallas_call(
        kernel,
        out_shape=out_shape,
        in_specs=[scalar if i < scalars else vmem for i in range(len(args))],
        out_specs=jax.tree.map(lambda _: vmem, out_shape),
        scratch_shapes=list(scratch),
        cost_estimate=pl.CostEstimate(flops=flops, bytes_accessed=0, transcendentals=0),
        compiler_params=pltpu.CompilerParams(vmem_limit_bytes=40 << 20),
    )(*args)


def swap(x, axis):
    return lax.ppermute(x, axis, [(0, 1), (1, 0)])


def per_device(frames, basis):
    rows, width = frames.shape
    vecs = basis.shape[1]
    n_time, n_feat = lax.axis_size(TIME), lax.axis_size(FEAT)
    n_z = lax.axis_size("z")
    block, part = lax.axis_index(TIME), lax.axis_index(FEAT)
    frames_counted = 2.0 * rows * (n_time - 1)
    count = jnp.where((block == 0) | (block == n_time - 1), 1.0, 2.0)
    f32, bf16 = jnp.float32, jnp.bfloat16

    piece = rows // n_feat
    owned = width // n_time
    steps = 4
    packed = pl.pallas_call(
        project_kernel,
        grid=(steps,),
        in_specs=[
            pl.BlockSpec((rows // steps, width), lambda i: (i, 0)),
            pl.BlockSpec((width, vecs), lambda i: (0, 0)),
        ],
        out_specs=pl.BlockSpec((n_feat, piece + 8, vecs), lambda i: (0, 0, 0)),
        out_shape=jax.ShapeDtypeStruct((n_feat, piece + 8, vecs), f32),
        compiler_params=pltpu.CompilerParams(vmem_limit_bytes=56 << 20),
    )(frames, basis)
    shift = call(shift_kernel, jax.ShapeDtypeStruct((n_time, 128), f32), frames)
    packed = lax.all_to_all(packed, FEAT, 0, 0, tiled=True)

    centred, offset = call(
        collect_kernel,
        [
            jax.ShapeDtypeStruct((n_feat, piece, vecs), bf16),
            jax.ShapeDtypeStruct((8, vecs), f32),
        ],
        packed,
    )
    centred = lax.all_to_all(centred, FEAT, 0, 0, tiled=True).reshape(rows, vecs)
    pairs = [(i, i + 1) for i in range(1, n_time - 1, 2)]
    across_chips = lax.ppermute(centred, TIME, pairs + [(b, a) for a, b in pairs])
    on_chip = swap(centred, "core")

    gram_rows = 2 * vecs // n_feat
    each = gram_rows // n_time
    cols = vecs // n_feat
    wide = vecs - (-(2 * cols + owned) // 128) * 128
    sent, beside = call(
        gram_kernel,
        [
            jax.ShapeDtypeStruct((n_time, each, wide), f32),
            jax.ShapeDtypeStruct((8, vecs), f32),
        ],
        jnp.stack([part, jnp.int32(n_feat), count.astype(jnp.int32)]),
        centred,
        on_chip,
        across_chips,
        offset,
        shift,
        scalars=1,
        scratch=[pltpu.VMEM((vecs, vecs), f32)],
    )
    got = lax.all_to_all(sent, TIME, 0, 0, tiled=True)
    gram, sums, shifts = call(
        total_kernel,
        [
            jax.ShapeDtypeStruct((n_time, each, vecs), f32),
            jax.ShapeDtypeStruct((n_time, 2 * cols), f32),
            jax.ShapeDtypeStruct((n_time, owned), f32),
        ],
        got,
    )
    gram = lax.all_to_all(gram, TIME, 0, 0, tiled=True)
    slices = call(
        slices_kernel,
        jax.ShapeDtypeStruct((n_feat, gram_rows, wide), f32),
        gram,
        sums,
    )
    slices = lax.all_to_all(slices, FEAT, 0, 0, tiled=True)

    half = jax.ShapeDtypeStruct((2 * n_z, owned, vecs), f32)
    kept, given = call(
        contract_kernel,
        [half, half],
        lax.axis_index("core")[None],
        frames,
        on_chip,
        across_chips,
        beside,
        scalars=1,
        scratch=[pltpu.VMEM((2 * n_z, 2, owned, vecs), f32)],
        flops=4 * rows * width * vecs,
    )
    half = jax.ShapeDtypeStruct((n_z, owned, vecs), f32)
    mine, given = call(
        halve_kernel,
        [half, half],
        lax.axis_index("xlo")[None],
        kept,
        swap(given, "core"),
        scalars=1,
    )
    lagged = (mine + swap(given, "xlo")).astype(bf16)
    lagged = lax.all_to_all(lagged, "z", 0, 0, tiled=True)

    square = jax.ShapeDtypeStruct((vecs, vecs), f32)
    inv, reduced, edge, share = call(
        lambda *refs: whiten_kernel(n_time, frames_counted, *refs),
        [
            square,
            square,
            jax.ShapeDtypeStruct((n_time, vecs), f32),
            jax.ShapeDtypeStruct((n_time, 128), f32),
        ],
        slices,
        flops=11 * 10**9,
    )
    new_basis = call(
        lambda *refs: finish_kernel(frames_counted, *refs),
        jax.ShapeDtypeStruct((owned, vecs), f32),
        lagged,
        shifts,
        edge,
        share,
        inv,
        flops=10**9,
    )
    return (new_basis, reduced)


def solution(mesh):
    n_time, n_feat = mesh.devices.shape
    mesh = Mesh(mesh.devices.reshape(2, n_time // 4, 2, 2, n_feat // 2), TIME + FEAT)
    return jax.shard_map(
        per_device,
        mesh=mesh,
        in_specs=(P(TIME, FEAT), P(FEAT, None)),
        out_specs=(P(FEAT + TIME, None), P()),
        check_vma=False,
    )
```

time: 185 us -> 148 us (0.80)
  blocking collectives: 28 us -> 52.8 us
  waiting for transfers between devices: 53.7 us -> 31.2 us
  between operations: 14.3 us -> 0.77 us
  matrix products: 7.06 us -> 0 us
  starting transfers between devices: 42 us -> 35.7 us
  other arithmetic: 5.5 us -> 0.84 us
  local copies, waits for them, and re-layouts: 5.01 us -> 0.95 us
  Pallas kernels: 28.1 us -> 25 us
    all_to_all x2 -> x3, blocking collectives: 28 us -> 52.8 us  [the longest x1 24.7 us: per_device(): got = lax.all_to_all(sent, TIME, 0, 0, tiled=True)]
    reduce_scatter x1 -> x0, waiting for transfers between devices: 12.3 us -> none  [per_device(): lax.psum_scatter(lagged.reshape(n_z * owned, vecs), 'z', scatter_dimensio...]
    all_to_all x3, waiting for transfers between devices: 38.8 us -> 28 us  [the longest x1 11.2 us: per_device(): slices = lax.all_to_all(slices, FEAT, 0, 0, tiled=True)]
    all_to_all x3, starting transfers between devices: 27.2 us -> 17.9 us  [the longest x1 6.3 us: per_device(): slices = lax.all_to_all(slices, FEAT, 0, 0, tiled=True)]
    dot_general x4 -> x0, matrix products: 7.06 us -> none  [dot(): lax.dot_general(a, b, (dims, ((), ())), precision=precision, preferred_el...]
    pallas_call x2 -> x10, Pallas kernels: 28.1 us -> 25 us  [the longest x9 20.5 us: call(): pl.pallas_call(kernel, out_shape=out_shape, in_specs=[scalar if i < scala...]
    ppermute x2 -> x3, starting transfers between devices: 3.84 us -> 6.07 us  [swap(): return lax.ppermute(x, axis, [(0, 1), (1, 0)])]
    reduce_sum x5 -> x0, other arithmetic: 2.21 us -> none  [the longest x1 1.03 us: per_device(): jnp.sum(earlier.astype(f32), axis=0)]
  transfers between devices with their start and end apart: 8 -> 7, of which waited for: 6 -> 4; matrix products, arithmetic and copies ran while one was open for 5% -> 1% of each run, Pallas kernels for 15% -> 10%
where the time goes in v2:
time: 148 us; the launch traced here: 147 us
  blocking collectives  52.8 us (36%)
  starting transfers between devices  35.7 us (24%)
  waiting for transfers between devices  31.2 us (21%)
  Pallas kernels  25 us (17%)
    all_to_all x1, blocking collectives, per_device(): got = lax.all_to_all(sent, TIME, 0, 0, tiled=True)  24.7 us
    pallas_call x9, Pallas kernels, call(): pl.pallas_call(kernel, out_shape=out_shape, in_specs=[scalar if i < scala...  20.5 us
    all_to_all x1, blocking collectives, per_device(): packed = lax.all_to_all(packed, FEAT, 0, 0, tiled=True)  16.9 us
    ppermute x1, starting transfers between devices, per_device(): lax.ppermute(centred, TIME, pairs + [(b, a) for a, b in pairs])  11.8 us
    all_to_all x1, waiting for transfers between devices, per_device(): slices = lax.all_to_all(slices, FEAT, 0, 0, tiled=True)  11.2 us
    all_to_all x1, blocking collectives, per_device(): lax.all_to_all(centred, FEAT, 0, 0, tiled=True).reshape(rows, vecs)  11.2 us
    all_to_all x1, waiting for transfers between devices, per_device(): gram = lax.all_to_all(gram, TIME, 0, 0, tiled=True)  10.1 us
    all_to_all x1, waiting for transfers between devices, per_device(): lagged = lax.all_to_all(lagged, 'z', 0, 0, tiled=True)  6.67 us
  transfers between devices with their start and end apart: 7, of which 4 were waited for; matrix products, arithmetic and copies ran while one was open for 1% of the time, Pallas kernels for 10%

profile of v2, /device:TPU:6, one launch (start us, length us, event | category | flops | bytes accessed | tf_op | source)
XLA Modules:
  0.0 147.2 jit_solution(4245563379923180058)
XLA Ops:
  0.6 0.0 copy-start
  0.6 4.5 %shard_map.41 = f32[8,72,256]{2,1,0:T(8,128)} custom-call(bf16[512,2048]{1,0:T(8,128)(2,1)} %frames_ref.5, bf16[2048,256]{1,0:T(8,128)(2,1)} %basis_ref.1), custom_call_target="tpu_custom_call" | custom-call | tf_op jit(solution)/shard_map/pallas_call | solution.py:288
  5.1 16.9 %all_to_all.30.got_ref = f32[8,72,256]{2,1,0:T(8,128)S(1)} all-to-all(f32[8,72,256]{2,1,0:T(8,128)} %shard_map.41), channel_id=1, replica_groups=mesh['xlo'=2,'z'=16,'core'=2,'xhi'=2,'y'=4] {'xhi','y'}, dimensions={0} | all-to-all | bytes 1179648 | tf_op jit(solution)/shard_map/all_to_all | solution.py:300
  22.0 11.2 %all_to_all.31 = bf16[8,64,256]{2,1,0:T(8,128)(2,1)S(1)} all-to-all(bf16[8,64,256]{2,1,0:T(8,128)(2,1)S(1)} %get-tuple-element.17), channel_id=1, replica_groups=mesh['xlo'=2,'z'=16,'core'=2,'xhi'=2,'y'=4] {'xhi','y'}, dimensions={0} | all-to-all | bytes 524288 | tf_op jit(solution)/shard_map/all_to_all | solution.py:310
  33.2 1.9 %collective-permute-start = (bf16[512,256]{1,0:T(8,128)(2,1)S(1)}, bf16[512,256]{1,0:T(8,128)(2,1)S(1)}, u32[]{:S(2)}, u32[]{:S(2)}) collective-permute-start(bf16[512,256]{1,0:T(8,128)(2,1)S(1)} %bitcast.5), channel_id=1, source_target_pairs={{0,8},{8,0},{1,9},{9,1},{2,10},{10,2},{3,11},{11,3},{4,12},{12,4},... | collective-permute-start | bytes 786440 | tf_op jit(solution)/shard_map/ppermute | solution.py:272
  35.2 11.8 %collective-permute-start.1 = (bf16[512,256]{1,0:T(8,128)(2,1)S(1)}, bf16[512,256]{1,0:T(8,128)(2,1)S(1)}, u32[]{:S(2)}, u32[]{:S(2)}) collective-permute-start(bf16[512,256]{1,0:T(8,128)(2,1)S(1)} %bitcast.6), channel_id=1, source_target_pairs={{8,16},{24,32},{40,48},{56,64},{72,80},{88,96},{104,112},{120,128}... | collective-permute-start | bytes 786440 | tf_op jit(solution)/shard_map/ppermute | solution.py:312
  46.9 0.0 copy-done
  46.9 0.8 shard_map.43.shift_ref
  47.7 0.1 pad_add_fusion.place_ref
  47.8 0.0 collective-permute-done.first_ref
  47.8 3.1 %collective-permute-done.1.second_ref = bf16[512,256]{1,0:T(8,128)(2,1)S(1)} collective-permute-done((bf16[512,256]{1,0:T(8,128)(2,1)S(1)}, bf16[512,256]{1,0:T(8,128)(2,1)S(1)}, u32[]{:S(2)}, u32[]{:S(2)}) %collective-permute-start.1) | collective-permute-done | bytes 262176 | tf_op jit(solution)/shard_map/ppermute | solution.py:312
  51.0 0.0 copy-start.1
  51.0 1.2 shard_map.44
  52.2 0.0 copy-done.1
  52.2 0.0 copy-start.2
  52.2 0.9 copy-done.2
  53.2 3.0 %shard_map.45 = (f32[32,32,256]{2,1,0:T(8,128)S(1)}, f32[32,32,256]{2,1,0:T(8,128)}) custom-call(s32[1]{0:T(128)} %bitcast.1.core_ref, bf16[512,2048]{1,0:T(8,128)(2,1)S(1)} %copy-done, bf16[512,256]{1,0:T(8,128)(2,1)S(1)} %collective-permute-done.first_ref, bf16[512,256]{1,0:T(8,128)(2,1)S(1)} %copy-done.2, f32[8,256]{1,0:T(8,128)S(1)} %get-tuple-element.19.beside_ref), custom_call_target="tpu_custom_call" | custom-call | flops 1073741824 | tf_op jit(solution)/shard_map/pallas_call | solution.py:260
  56.2 1.9 %collective-permute-start.2 = (f32[32,32,256]{2,1,0:T(8,128)}, f32[32,32,256]{2,1,0:T(8,128)S(1)}, u32[]{:S(2)}, u32[]{:S(2)}) collective-permute-start(f32[32,32,256]{2,1,0:T(8,128)} %get-tuple-element.21), channel_id=1, source_target_pairs={{0,8},{8,0},{1,9},{9,1},{2,10},{10,2},{3,11},{11,3},{4,12},{12,4},... | collective-permute-start | bytes 3145736 | tf_op jit(solution)/shard_map/ppermute | solution.py:272
  58.1 24.7 %all_to_all.32.got_ref = f32[64,1,384]{2,1,0:T(1,128)S(1)} all-to-all(f32[64,1,384]{2,1,0:T(1,128)S(1)} %get-tuple-element.24), channel_id=1, replica_groups=mesh['xlo'=2,'z'=16,'core'=2,'xhi'=2,'y'=4] {'xlo','z','core'}, dimensions={0} | all-to-all | bytes 196608 | tf_op jit(solution)/shard_map/all_to_all | solution.py:334
  82.8 0.7 shard_map.47
  83.5 5.9 %all-to-all-start.4 = ((f32[64,1,256]{2,1,0:T(1,128)}), f32[64,1,256]{2,1,0:T(1,128)S(1)}, u32[]{:S(2)}, u32[]{:S(2)}) async-start(f32[64,1,256]{2,1,0:T(1,128)} %get-tuple-element.26), calls=%async_computation.4 | async-start | bytes 131072 | tf_op jit(solution)/shard_map/all_to_all | solution.py:344
  89.4 0.0 collective-permute-done.2.got_ref
  89.4 0.9 shard_map.46
  90.4 2.3 %collective-permute-start.3 = (f32[16,32,256]{2,1,0:T(8,128)}, f32[16,32,256]{2,1,0:T(8,128)S(1)}, u32[]{:S(2)}, u32[]{:S(2)}) collective-permute-start(f32[16,32,256]{2,1,0:T(8,128)} %get-tuple-element.23), channel_id=1, source_target_pairs={{0,256},{256,0},{1,257},{257,1},{2,258},{258,2},{3,259},{259,3},{4... | collective-permute-start | bytes 1572872 | tf_op jit(solution)/shard_map/ppermute | solution.py:272
  92.6 10.1 %all-to-all-done.4.rows_ref = f32[64,1,256]{2,1,0:T(1,128)S(1)} async-done(((f32[64,1,256]{2,1,0:T(1,128)}), f32[64,1,256]{2,1,0:T(1,128)S(1)}, u32[]{:S(2)}, u32[]{:S(2)}) %all-to-all-start.4) | async-done | bytes 65568 | tf_op jit(solution)/shard_map/all_to_all | solution.py:344
  102.7 1.0 shard_map.48
  103.7 6.3 %all-to-all-start.5 = ((f32[8,64,384]{2,1,0:T(8,128)}), f32[8,64,384]{2,1,0:T(8,128)S(1)}, u32[]{:S(2)}, u32[]{:S(2)}) async-start(f32[8,64,384]{2,1,0:T(8,128)} %shard_map.48), calls=%async_computation.5 | async-start | bytes 1572864 | tf_op jit(solution)/shard_map/all_to_all | solution.py:351
  110.0 0.0 collective-permute-done.3
  110.0 0.8 add_convert_fusion
  110.8 11.2 %all-to-all-done.5.refs_0_ = f32[8,64,384]{2,1,0:T(8,128)S(1)} async-done(((f32[8,64,384]{2,1,0:T(8,128)}), f32[8,64,384]{2,1,0:T(8,128)S(1)}, u32[]{:S(2)}, u32[]{:S(2)}) %all-to-all-start.5) | async-done | bytes 786464 | tf_op jit(solution)/shard_map/all_to_all | solution.py:351
  122.0 5.7 %all-to-all-start.2 = ((bf16[16,32,256]{2,1,0:T(8,128)(2,1)}), bf16[16,32,256]{2,1,0:T(8,128)(2,1)S(1)}, u32[]{:S(2)}, u32[]{:S(2)}) async-start(bf16[16,32,256]{2,1,0:T(8,128)(2,1)} %add_convert_fusion), calls=%async_computation.2 | async-start | bytes 524288 | tf_op jit(solution)/shard_map/all_to_all | solution.py:376
  127.7 11.7 %shard_map.49 = (f32[256,256]{1,0:T(8,128)S(1)}, f32[256,256]{1,0:T(8,128)}, f32[64,256]{1,0:T(8,128)S(1)}, f32[64,128]{1,0:T(8,128)S(1)}) custom-call(f32[8,64,384]{2,1,0:T(8,128)S(1)} %all-to-all-done.5.refs_0_), custom_call_target="tpu_custom_call" | custom-call | flops 11000000512 | tf_op jit(solution)/shard_map/pallas_call | solution.py:260
  139.4 6.7 %all-to-all-done.2.refs_0_ = bf16[16,32,256]{2,1,0:T(8,128)(2,1)S(1)} async-done(((bf16[16,32,256]{2,1,0:T(8,128)(2,1)}), bf16[16,32,256]{2,1,0:T(8,128)(2,1)S(1)}, u32[]{:S(2)}, u32[]{:S(2)}) %all-to-all-start.2) | async-done | bytes 262176 | tf_op jit(solution)/shard_map/all_to_all | solution.py:376
  146.0 1.2 shard_map.50
  (1 shorter events, 0.0 us)
Async XLA Ops:
  0.6 46.3 %copy-start = (bf16[512,2048]{1,0:T(8,128)(2,1)S(1)}, bf16[512,2048]{1,0:T(8,128)(2,1)}, u32[]{:S(2)}) copy-start(bf16[512,2048]{1,0:T(8,128)(2,1)} %frames_ref.5) | copy-start | bytes 6291460
  33.2 14.6 %collective-permute-start = (bf16[512,256]{1,0:T(8,128)(2,1)S(1)}, bf16[512,256]{1,0:T(8,128)(2,1)S(1)}, u32[]{:S(2)}, u32[]{:S(2)}) collective-permute-start(bf16[512,256]{1,0:T(8,128)(2,1)S(1)} %bitcast.5), channel_id=1, source_target_pairs={{0,8},{8,0},{1,9},{9,1},{2,10},{10,2},{3,11},{11,3},{4,12},{12,4},... | collective-permute-start | bytes 786440 | tf_op jit(solution)/shard_map/ppermute | solution.py:272
  35.2 15.8 %collective-permute-start.1 = (bf16[512,256]{1,0:T(8,128)(2,1)S(1)}, bf16[512,256]{1,0:T(8,128)(2,1)S(1)}, u32[]{:S(2)}, u32[]{:S(2)}) collective-permute-start(bf16[512,256]{1,0:T(8,128)(2,1)S(1)} %bitcast.6), channel_id=1, source_target_pairs={{8,16},{24,32},{40,48},{56,64},{72,80},{88,96},{104,112},{120,128}... | collective-permute-start | bytes 786440 | tf_op jit(solution)/shard_map/ppermute | solution.py:312
  51.0 1.2 copy-start.1
  52.2 1.0 copy-start.2
  56.2 33.2 %collective-permute-start.2 = (f32[32,32,256]{2,1,0:T(8,128)}, f32[32,32,256]{2,1,0:T(8,128)S(1)}, u32[]{:S(2)}, u32[]{:S(2)}) collective-permute-start(f32[32,32,256]{2,1,0:T(8,128)} %get-tuple-element.21), channel_id=1, source_target_pairs={{0,8},{8,0},{1,9},{9,1},{2,10},{10,2},{3,11},{11,3},{4,12},{12,4},... | collective-permute-start | bytes 3145736 | tf_op jit(solution)/shard_map/ppermute | solution.py:272
  83.5 19.2 %all-to-all-start.4 = ((f32[64,1,256]{2,1,0:T(1,128)}), f32[64,1,256]{2,1,0:T(1,128)S(1)}, u32[]{:S(2)}, u32[]{:S(2)}) async-start(f32[64,1,256]{2,1,0:T(1,128)} %get-tuple-element.26), calls=%async_computation.4 | async-start | bytes 131072 | tf_op jit(solution)/shard_map/all_to_all | solution.py:344
  90.4 19.6 %collective-permute-start.3 = (f32[16,32,256]{2,1,0:T(8,128)}, f32[16,32,256]{2,1,0:T(8,128)S(1)}, u32[]{:S(2)}, u32[]{:S(2)}) collective-permute-start(f32[16,32,256]{2,1,0:T(8,128)} %get-tuple-element.23), channel_id=1, source_target_pairs={{0,256},{256,0},{1,257},{257,1},{2,258},{258,2},{3,259},{259,3},{4... | collective-permute-start | bytes 1572872 | tf_op jit(solution)/shard_map/ppermute | solution.py:272
  103.7 18.3 %all-to-all-start.5 = ((f32[8,64,384]{2,1,0:T(8,128)}), f32[8,64,384]{2,1,0:T(8,128)S(1)}, u32[]{:S(2)}, u32[]{:S(2)}) async-start(f32[8,64,384]{2,1,0:T(8,128)} %shard_map.48), calls=%async_computation.5 | async-start | bytes 1572864 | tf_op jit(solution)/shard_map/all_to_all | solution.py:351
  122.0 24.0 %all-to-all-start.2 = ((bf16[16,32,256]{2,1,0:T(8,128)(2,1)}), bf16[16,32,256]{2,1,0:T(8,128)(2,1)S(1)}, u32[]{:S(2)}, u32[]{:S(2)}) async-start(bf16[16,32,256]{2,1,0:T(8,128)(2,1)} %add_convert_fusion), calls=%async_computation.2 | async-start | bytes 524288 | tf_op jit(solution)/shard_map/all_to_all | solution.py:376

commit v3 on v2

--- a/solution.py
+++ b/solution.py
@@ -5,7 +5,7 @@
 from jax.experimental.pallas import tpu as pltpu
 from jax.sharding import Mesh, PartitionSpec as P
 
-TIME = ("xlo", "z", "core")
+TIME = ("xlo", "zh", "zl", "core")
 FEAT = ("xhi", "y")
 EXACT = lax.Precision.HIGHEST
 
@@ -77,16 +77,33 @@
 
 
 def whiten_kernel(blocks, frames_counted, g_ref, inv_ref, reduced_ref, edge_ref, mean_ref):
-    n_feat, rows, wide = g_ref.shape
-    vecs = n_feat * rows // 2
-    part = vecs // n_feat
-    half = n_feat // 2
-    gram0 = jnp.concatenate([g_ref[k, :, :vecs] for k in range(half)], axis=0)
-    gram1 = jnp.concatenate([g_ref[half + k, :, :vecs] for k in range(half)], axis=0)
-    u = jnp.concatenate([g_ref[k, :blocks, vecs : vecs + part] for k in range(n_feat)], axis=1)
-    z = jnp.concatenate(
-        [g_ref[k, :blocks, vecs + part : vecs + 2 * part] for k in range(n_feat)], axis=1
-    )
+    peers, height, vecs = g_ref.shape
+    n_feat, rows = peers // 2, height - 8
+    part, half = vecs // n_feat, n_feat // 2
+
+    def joined(start):
+        return jnp.concatenate(
+            [g_ref[x * n_feat + start + k, :rows] for k in range(half) for x in range(2)], axis=0
+        )
+
+    def sums(start):
+        columns = []
+        for k in range(n_feat):
+            side = [g_ref[x * n_feat + k, rows:] for x in range(2)]
+            columns.append(
+                jnp.concatenate(
+                    [
+                        side[x][:, 2 * part * g + start : 2 * part * g + start + part]
+                        for x in range(2)
+                        for g in range(blocks // 16)
+                    ],
+                    axis=0,
+                )
+            )
+        return jnp.concatenate(columns, axis=1)
+
+    gram0, gram1 = joined(0), joined(half)
+    u, z = sums(0), sums(part)
     size = frames_counted / (2.0 * blocks - 2.0)
     ids = lax.broadcasted_iota(jnp.int32, (blocks, 1), 0)
     count = jnp.where((ids == 0) | (ids == blocks - 1), 1.0, 2.0)
@@ -116,22 +133,6 @@
     out_ref[...] = dot(lagged / frames_counted, inv_ref[...], ((1,), (1,)))
 
 
-def project_kernel(frames_ref, basis_ref, packed_ref):
-    step, steps = pl.program_id(0), pl.num_programs(0)
-    pieces, tall, vecs = packed_ref.shape
-    piece = tall - 8
-    each = pieces // steps
-    block = dot(frames_ref[...], basis_ref[...], precision=None)
-    packed_ref[pl.ds(step * each, each), :piece] = block.reshape(each, piece, vecs)
-
-    @pl.when(step == steps - 1)
-    def _():
-        values = packed_ref[:, :piece]
-        local = jnp.sum(jnp.sum(values, axis=0), axis=0, keepdims=True) / (pieces * piece)
-        packed_ref[:, :piece] = values - local[None]
-        packed_ref[:, piece:] = jnp.broadcast_to(local[None], (pieces, 8, vecs))
-
-
 def shift_kernel(frames_ref, out_ref):
     n_time, lanes = out_ref.shape
     rows, width = frames_ref.shape
@@ -150,8 +151,9 @@
 
 def collect_kernel(got_ref, centred_ref, offset_ref):
     piece = centred_ref.shape[1]
-    total = jnp.sum(got_ref[...], axis=0)
-    offset_ref[...] = total[piece:]
+    total = jnp.sum(got_ref[...].astype(jnp.float32), axis=0)
+    offset = jnp.sum(total[piece:], axis=0, keepdims=True)
+    offset_ref[...] = jnp.broadcast_to(offset, offset_ref.shape)
     centred_ref[...] = jnp.broadcast_to(total[:piece].astype(jnp.bfloat16)[None], centred_ref.shape)
 
 
@@ -163,7 +165,7 @@
     part, n_feat, count = place_ref[0], place_ref[1], place_ref[2]
     half = n_feat // 2
     across = ((0,), (0,))
-    first, second = first_ref[...], second_ref[...]
+    first, second = first_ref[1 - place_ref[3]], second_ref[...]
     beside = jnp.sum(first.astype(jnp.float32), axis=0, keepdims=True) + jnp.sum(
         second.astype(jnp.float32), axis=0, keepdims=True
     )
@@ -203,68 +205,76 @@
 
 
 def total_kernel(got_ref, row_ref, sums_ref, shift_ref):
-    n_time, each, vecs = row_ref.shape
+    copies, _, vecs = row_ref.shape
+    n_time = sums_ref.shape[0]
     total = got_ref[0, :, :vecs]
     for i in range(1, n_time):
         total = total + got_ref[i, :, :vecs]
+    for i in range(copies):
+        row_ref[i] = total
     low = vecs + sums_ref.shape[1]
     for i in range(n_time):
-        row_ref[i] = total
         sums_ref[i : i + 1] = got_ref[i, :1, vecs:low]
         shift_ref[i : i + 1] = got_ref[i, :1, low : low + shift_ref.shape[1]]
 
 
-def slices_kernel(rows_ref, sums_ref, out_ref):
-    n_feat, height, wide = out_ref.shape
-    n_time, each, vecs = rows_ref.shape
-    for i in range(n_time):
-        out_ref[0, i * each : (i + 1) * each, :vecs] = rows_ref[i]
-    side = jnp.zeros((n_time, wide - vecs - sums_ref.shape[1]), jnp.float32)
-    out_ref[0, :n_time, vecs:] = jnp.concatenate([sums_ref[...], side], axis=1)
-    if height > n_time:
-        out_ref[0, n_time:, vecs:] = jnp.zeros((height - n_time, wide - vecs), jnp.float32)
-    for k in range(1, n_feat):
+def slices_kernel(xlo_ref, rows_ref, sums_ref, _, out_ref):
+    copies, height, vecs = out_ref.shape
+    blocks, each, _ = rows_ref.shape
+    for i in range(blocks):
+        out_ref[0, i * each : (i + 1) * each] = rows_ref[i]
+    first = pl.multiple_of(xlo_ref[0] * blocks, 8)
+    side = [sums_ref[pl.ds(first + 8 * g, 8), :] for g in range(blocks // 8)]
+    rest = vecs - len(side) * sums_ref.shape[1]
+    side = side + [jnp.zeros((8, rest), jnp.float32)] if rest else side
+    out_ref[0, height - 8 :] = jnp.concatenate(side, axis=1)
+    for k in range(1, copies):
         out_ref[k] = out_ref[0]
 
 
-def contract_kernel(core_ref, frames_ref, first_ref, second_ref, beside_ref, kept_ref, given_ref, all_ref):
-    owned = kept_ref.shape[1]
+def contract_kernel(core_ref, frames_ref, first_ref, second_ref, beside_ref, kept_ref, given_ref):
+    owned, vecs = kept_ref.shape[1:]
     rows, width = frames_ref.shape
-    step = 8 * owned
-    across = ((0,), (0,))
+    groups = 4
+    core = core_ref[0]
     beside = beside_ref[:1] / rows
-    ones = jnp.ones((rows, 128), jnp.bfloat16)
+    right = jnp.concatenate(
+        [first_ref[1 - core], second_ref[...], jnp.ones((rows, 128), jnp.bfloat16)], axis=1
+    )
+    step = 2 * groups * owned
     for i in range(width // step):
-        frames = frames_ref[:, i * step : (i + 1) * step]
-        sums = dot(frames, first_ref[...], across, None) + dot(frames, second_ref[...], across, None)
-        total = dot(frames, ones, across, None)
-        total = jnp.concatenate([total] * (sums.shape[1] // 128), axis=1)
-        sums = sums - total * beside
-        all_ref[4 * i : 4 * i + 4] = sums.reshape(4, 2, owned, sums.shape[1])
-    core = core_ref[0]
-    kept_ref[...] = all_ref[:, core]
-    given_ref[...] = all_ref[:, 1 - core]
-
-
-def halve_kernel(xlo_ref, kept_ref, got_ref, mine_ref, given_ref):
-    xlo = xlo_ref[0]
-    half = mine_ref.shape[0]
-    own, other = pl.ds(xlo * half, half), pl.ds((1 - xlo) * half, half)
-    mine_ref[...] = kept_ref[own] + got_ref[own]
-    given_ref[...] = kept_ref[other] + got_ref[other]
-
-
-def call(kernel, out_shape, *args, scalars=0, scratch=(), flops=0):
+        sums = dot(frames_ref[:, i * step : (i + 1) * step], right, ((0,), (0,)), None)
+        total = jnp.concatenate([sums[:, 2 * vecs :]] * (vecs // 128), axis=1)
+        sums = sums[:, :vecs] + sums[:, vecs : 2 * vecs] - total * beside
+        sums = sums.reshape(groups, 2, owned, vecs)
+        low, high = sums[:, 0], sums[:, 1]
+        part = slice(i * groups, (i + 1) * groups)
+        kept_ref[part] = jnp.where(core == 0, low, high)
+        given_ref[part] = jnp.where(core == 0, high, low).astype(given_ref.dtype)
+
+
+def halve_kernel(axis, place_ref, kept_ref, got_ref, mine_ref, given_ref):
+    def at(which):
+        return (slice(None),) * axis + (which,)
+
+    own, other = at(place_ref[0]), at(1 - place_ref[0])
+    mine_ref[...] = kept_ref[own] + got_ref[own].astype(jnp.float32)
+    given_ref[...] = (kept_ref[other] + got_ref[other].astype(jnp.float32)).astype(given_ref.dtype)
+
+
+def call(kernel, out_shape, *args, scalars=0, unread=0, scratch=(), flops=0):
     vmem = pl.BlockSpec(memory_space=pltpu.VMEM)
     scalar = pl.BlockSpec(memory_space=pltpu.SMEM)
     return pl.pallas_call(
         kernel,
         out_shape=out_shape,
-        in_specs=[scalar if i < scalars else vmem for i in range(len(args))],
+        in_specs=[scalar] * scalars
+        + [vmem] * (len(args) - scalars - unread)
+        + [pl.BlockSpec(memory_space=pl.ANY)] * unread,
         out_specs=jax.tree.map(lambda _: vmem, out_shape),
         scratch_shapes=list(scratch),
         cost_estimate=pl.CostEstimate(flops=flops, bytes_accessed=0, transcendentals=0),
-        compiler_params=pltpu.CompilerParams(vmem_limit_bytes=40 << 20),
+        compiler_params=pltpu.CompilerParams(vmem_limit_bytes=20 << 20),
     )(*args)
 
 
@@ -276,26 +286,30 @@
     rows, width = frames.shape
     vecs = basis.shape[1]
     n_time, n_feat = lax.axis_size(TIME), lax.axis_size(FEAT)
-    n_z = lax.axis_size("z")
+    n_z = 2 * lax.axis_size("zh")
     block, part = lax.axis_index(TIME), lax.axis_index(FEAT)
     frames_counted = 2.0 * rows * (n_time - 1)
     count = jnp.where((block == 0) | (block == n_time - 1), 1.0, 2.0)
     f32, bf16 = jnp.float32, jnp.bfloat16
 
+    core, xlo = lax.axis_index("core"), lax.axis_index("xlo")
+
     piece = rows // n_feat
     owned = width // n_time
-    steps = 4
-    packed = pl.pallas_call(
-        project_kernel,
-        grid=(steps,),
-        in_specs=[
-            pl.BlockSpec((rows // steps, width), lambda i: (i, 0)),
-            pl.BlockSpec((width, vecs), lambda i: (0, 0)),
-        ],
-        out_specs=pl.BlockSpec((n_feat, piece + 8, vecs), lambda i: (0, 0, 0)),
-        out_shape=jax.ShapeDtypeStruct((n_feat, piece + 8, vecs), f32),
-        compiler_params=pltpu.CompilerParams(vmem_limit_bytes=56 << 20),
-    )(frames, basis)
+    projected = dot(frames, basis, precision=None)
+    local = jnp.mean(projected, axis=0)
+    high = lax.reduce_precision(local, 8, 7)
+    middle = lax.reduce_precision(local - high, 8, 7)
+    low = local - high - middle
+    terms = jnp.stack([high, middle, low]).astype(bf16)
+    terms = jnp.concatenate([terms, jnp.zeros((13, vecs), bf16)], axis=0)
+    packed = jnp.concatenate(
+        [
+            (projected - local).astype(bf16).reshape(n_feat, piece, vecs),
+            jnp.broadcast_to(terms, (n_feat, 16, vecs)),
+        ],
+        axis=1,
+    )
     shift = call(shift_kernel, jax.ShapeDtypeStruct((n_time, 128), f32), frames)
     packed = lax.all_to_all(packed, FEAT, 0, 0, tiled=True)
 
@@ -310,7 +324,7 @@
     centred = lax.all_to_all(centred, FEAT, 0, 0, tiled=True).reshape(rows, vecs)
     pairs = [(i, i + 1) for i in range(1, n_time - 1, 2)]
     across_chips = lax.ppermute(centred, TIME, pairs + [(b, a) for a, b in pairs])
-    on_chip = swap(centred, "core")
+    on_chip = lax.all_gather(centred, "core")
 
     gram_rows = 2 * vecs // n_feat
     each = gram_rows // n_time
@@ -322,7 +336,7 @@
             jax.ShapeDtypeStruct((n_time, each, wide), f32),
             jax.ShapeDtypeStruct((8, vecs), f32),
         ],
-        jnp.stack([part, jnp.int32(n_feat), count.astype(jnp.int32)]),
+        jnp.stack([part, jnp.int32(n_feat), count.astype(jnp.int32), core]),
         centred,
         on_chip,
         across_chips,
@@ -335,45 +349,60 @@
     gram, sums, shifts = call(
         total_kernel,
         [
-            jax.ShapeDtypeStruct((n_time, each, vecs), f32),
+            jax.ShapeDtypeStruct((n_time // 2, each, vecs), f32),
             jax.ShapeDtypeStruct((n_time, 2 * cols), f32),
             jax.ShapeDtypeStruct((n_time, owned), f32),
         ],
         got,
     )
-    gram = lax.all_to_all(gram, TIME, 0, 0, tiled=True)
-    slices = call(
-        slices_kernel,
-        jax.ShapeDtypeStruct((n_feat, gram_rows, wide), f32),
-        gram,
-        sums,
-    )
-    slices = lax.all_to_all(slices, FEAT, 0, 0, tiled=True)
-
-    half = jax.ShapeDtypeStruct((2 * n_z, owned, vecs), f32)
+    half = (2 * n_z, owned, vecs)
     kept, given = call(
         contract_kernel,
-        [half, half],
-        lax.axis_index("core")[None],
+        [jax.ShapeDtypeStruct(half, f32), jax.ShapeDtypeStruct(half, bf16)],
+        core[None],
         frames,
         on_chip,
         across_chips,
         beside,
         scalars=1,
-        scratch=[pltpu.VMEM((2 * n_z, 2, owned, vecs), f32)],
         flops=4 * rows * width * vecs,
     )
-    half = jax.ShapeDtypeStruct((n_z, owned, vecs), f32)
+    place = (2, n_z // 2, 2, owned, vecs)
     mine, given = call(
-        halve_kernel,
-        [half, half],
-        lax.axis_index("xlo")[None],
-        kept,
-        swap(given, "core"),
+        lambda *refs: halve_kernel(0, *refs),
+        [jax.ShapeDtypeStruct(place[1:], f32), jax.ShapeDtypeStruct(place[1:], bf16)],
+        xlo[None],
+        kept.reshape(place),
+        swap(given, "core").reshape(place),
         scalars=1,
     )
-    lagged = (mine + swap(given, "xlo")).astype(bf16)
-    lagged = lax.all_to_all(lagged, "z", 0, 0, tiled=True)
+
+    gram = lax.all_to_all(gram, ("zh", "zl", "core"), 0, 0, tiled=True)
+    slices = call(
+        slices_kernel,
+        jax.ShapeDtypeStruct((2 * n_feat, gram_rows // 2 + 8, vecs), f32),
+        xlo[None],
+        gram,
+        sums,
+        mine,
+        scalars=1,
+        unread=1,
+    )
+    slices = lax.all_to_all(slices, ("xlo",) + FEAT, 0, 0, tiled=True)
+
+    mine, given = call(
+        lambda *refs: halve_kernel(1, *refs),
+        [
+            jax.ShapeDtypeStruct((n_z // 2, owned, vecs), f32),
+            jax.ShapeDtypeStruct((n_z // 2, owned, vecs), bf16),
+        ],
+        lax.axis_index("zl")[None],
+        mine,
+        swap(given, "xlo"),
+        scalars=1,
+    )
+    lagged = (mine + swap(given, "zl").astype(f32)).astype(bf16)
+    lagged = lax.all_to_all(lagged, "zh", 0, 0, tiled=True)
 
     square = jax.ShapeDtypeStruct((vecs, vecs), f32)
     inv, reduced, edge, share = call(
@@ -402,7 +431,7 @@
 
 def solution(mesh):
     n_time, n_feat = mesh.devices.shape
-    mesh = Mesh(mesh.devices.reshape(2, n_time // 4, 2, 2, n_feat // 2), TIME + FEAT)
+    mesh = Mesh(mesh.devices.reshape(2, n_time // 8, 2, 2, 2, n_feat // 2), TIME + FEAT)
     return jax.shard_map(
         per_device,
         mesh=mesh,

time: 148 us -> 134 us (0.905)
  waiting for transfers between devices: 31.2 us -> 19.8 us
  starting transfers between devices: 35.7 us -> 30.8 us
  Pallas kernels: 25 us -> 20.8 us
  local copies, waits for them, and re-layouts: 0.95 us -> 3.44 us
  matrix products: 0 us -> 2.31 us
  blocking collectives: 52.8 us -> 54.8 us
    all_to_all x3, waiting for transfers between devices: 28 us -> 14.4 us  [the longest x1 8.1 us: per_device(): gram = lax.all_to_all(gram, ('zh', 'zl', 'core'), 0, 0, tiled=True)]
    ppermute x3, waiting for transfers between devices: 0.01 us -> 4.34 us  [swap(): return lax.ppermute(x, axis, [(0, 1), (1, 0)])]
    pallas_call x10, Pallas kernels: 25 us -> 20.8 us  [call(): pl.pallas_call(kernel, out_shape=out_shape, in_specs=[scalar] * scalars +...]
    all_to_all x3, starting transfers between devices: 17.9 us -> 13.9 us  [the longest x1 6.47 us: per_device(): slices = lax.all_to_all(slices, ('xlo',) + FEAT, 0, 0, tiled=True)]
    all_to_all x1, blocking collectives: 16.9 us -> 14 us  [per_device(): packed = lax.all_to_all(packed, FEAT, 0, 0, tiled=True)]
    ppermute x1, starting transfers between devices: 11.8 us -> 9.01 us  [per_device(): lax.ppermute(centred, TIME, pairs + [(b, a) for a, b in pairs])]
    all_to_all x1, blocking collectives: 24.7 us -> 27.5 us  [per_device(): got = lax.all_to_all(sent, TIME, 0, 0, tiled=True)]
    unnamed x6 -> x8, local copies, waits for them, and re-layouts: 0.95 us -> 3.44 us
  transfers between devices with their start and end apart: 7 -> 7, of which waited for: 4 -> 5; matrix products, arithmetic and copies ran while one was open for 1% -> 1% of each run, Pallas kernels for 10% -> 11%
where the time goes in v3:
time: 134 us
  blocking collectives  54.8 us (41%)
  starting transfers between devices  30.8 us (23%)
  Pallas kernels  20.8 us (16%)
  waiting for transfers between devices  19.8 us (15%)
  local copies, waits for them, and re-layouts  3.44 us (3%)
  matrix products  2.31 us (2%)
    all_to_all x1, blocking collectives, per_device(): got = lax.all_to_all(sent, TIME, 0, 0, tiled=True)  27.5 us
    pallas_call x10, Pallas kernels, call(): pl.pallas_call(kernel, out_shape=out_shape, in_specs=[scalar] * scalars +...  20.8 us
    all_to_all x1, blocking collectives, per_device(): packed = lax.all_to_all(packed, FEAT, 0, 0, tiled=True)  14 us
    all_to_all x1, blocking collectives, per_device(): lax.all_to_all(centred, FEAT, 0, 0, tiled=True).reshape(rows, vecs)  11.2 us
    ppermute x1, starting transfers between devices, per_device(): lax.ppermute(centred, TIME, pairs + [(b, a) for a, b in pairs])  9.01 us
    all_to_all x1, waiting for transfers between devices, per_device(): gram = lax.all_to_all(gram, ('zh', 'zl', 'core'), 0, 0, tiled=True)  8.1 us
    ppermute x3, starting transfers between devices, swap(): return lax.ppermute(x, axis, [(0, 1), (1, 0)])  7.94 us
    all_to_all x1, starting transfers between devices, per_device(): slices = lax.all_to_all(slices, ('xlo',) + FEAT, 0, 0, tiled=True)  6.47 us
  transfers between devices with their start and end apart: 7, of which 5 were waited for; matrix products, arithmetic and copies ran while one was open for 1% of the time, Pallas kernels for 11%

profile of v3, /device:TPU:6, one launch (start us, length us, event | category | flops | bytes accessed | tf_op | source)
XLA Modules:
  0.0 133.7 jit_solution(13914808769016248808)
XLA Ops:
  0.6 0.0 copy-start
  0.6 1.2 copy-done
  1.9 2.3 %fusion.6 = (f32[256]{0:T(256)S(1)}, f32[512,256]{1,0:T(8,128)S(1)}) fusion(bf16[512,2048]{1,0:T(8,128)(2,1)} %frames_ref.3, bf16[2048,256]{1,0:T(8,128)(2,1)S(1)} %copy-done), kind=kOutput, calls=%fused_computation.16 | convolution fusion | flops 537001728 | bytes 3671040 | tf_op jit(solution)/shard_map/dot_general | solution.py:14
  4.2 0.0 copy-start.1
  4.3 14.0 %all_to_all.30.got_ref = bf16[8,80,256]{2,1,0:T(8,128)(2,1)S(1)} all-to-all(bf16[8,80,256]{2,1,0:T(8,128)(2,1)S(1)} %pad_maximum_fusion), channel_id=1, replica_groups=mesh['xlo'=2,'zh'=8,'zl'=2,'core'=2,'xhi'=2,'y'=4] {'xhi','y'}, dimensions={0} | all-to-all | bytes 655360 | tf_op jit(solution)/shard_map/all_to_all | solution.py:314
  18.3 0.1 shard_map.41
  18.4 11.2 %all_to_all.31 = bf16[8,64,256]{2,1,0:T(8,128)(2,1)S(1)} all-to-all(bf16[8,64,256]{2,1,0:T(8,128)(2,1)S(1)} %get-tuple-element.19), channel_id=1, replica_groups=mesh['xlo'=2,'zh'=8,'zl'=2,'core'=2,'xhi'=2,'y'=4] {'xhi','y'}, dimensions={0} | all-to-all | bytes 524288 | tf_op jit(solution)/shard_map/all_to_all | solution.py:324
  29.6 9.0 %collective-permute-start = (bf16[512,256]{1,0:T(8,128)(2,1)S(1)}, bf16[512,256]{1,0:T(8,128)(2,1)}, u32[]{:S(2)}, u32[]{:S(2)}) collective-permute-start(bf16[512,256]{1,0:T(8,128)(2,1)S(1)} %bitcast.13), channel_id=1, source_target_pairs={{8,16},{24,32},{40,48},{56,64},{72,80},{88,96},{104,112},{120,128}... | collective-permute-start | bytes 786440 | tf_op jit(solution)/shard_map/ppermute | solution.py:326
  38.6 0.0 copy-done.1
  38.6 0.8 shard_map.42.shift_ref
  39.4 0.1 pad_add_fusion.place_ref
  39.5 2.2 %all_gather.3.first_ref = bf16[2,512,256]{2,1,0:T(8,128)(2,1)S(1)} all-gather(bf16[1,512,256]{2,1,0:T(8,128)(2,1)S(1)} %bitcast.14), channel_id=1, replica_groups=mesh['xlo'=2,'zh'=8,'zl'=2,'core'=2,'xhi'=2,'y'=4] {'core'}, dimensions={0}, use_global_device_ids=true | all-gather | bytes 786432 | tf_op jit(solution)/shard_map/all_gather | solution.py:327
  41.7 1.1 collective-permute-done.second_ref
  42.7 1.6 %shard_map.43 = (f32[64,1,384]{2,1,0:T(1,128)S(1)}, f32[8,256]{1,0:T(8,128)S(1)}) custom-call(s32[4]{0:T(128)S(1)} %pad_add_fusion.place_ref, bf16[512,256]{1,0:T(8,128)(2,1)S(1)} %bitcast.15, bf16[2,512,256]{2,1,0:T(8,128)(2,1)S(1)} %all_gather.3.first_ref, bf16[512,256]{1,0:T(8,128)(2,1)} %collective-permute-done.second_ref, ...), custom_call_target="tpu_custom_call" | custom-call | tf_op jit(solution)/shard_map/pallas_call | solution.py:268
  44.4 3.6 %shard_map.44 = (f32[32,32,256]{2,1,0:T(8,128)S(1)}, bf16[32,32,256]{2,1,0:T(8,128)(2,1)}) custom-call(s32[1]{0:T(128)} %bitcast.2.core_ref, bf16[512,2048]{1,0:T(8,128)(2,1)S(1)} %copy-done.1, bf16[2,512,256]{2,1,0:T(8,128)(2,1)S(1)} %all_gather.3.first_ref, bf16[512,256]{1,0:T(8,128)(2,1)} %collective-permute-done.second_ref, ...), custom_call_target="tpu_custom_call" | custom-call | flops 1073741824 | tf_op jit(solution)/shard_map/pallas_call | solution.py:268
  48.0 0.0 copy-start.2
  48.0 1.0 copy-done.2
  49.0 1.9 %collective-permute-start.1 = (bf16[32,32,256]{2,1,0:T(8,128)(2,1)}, bf16[32,32,256]{2,1,0:T(8,128)(2,1)S(1)}, u32[]{:S(2)}, u32[]{:S(2)}) collective-permute-start(bf16[32,32,256]{2,1,0:T(8,128)(2,1)} %get-tuple-element.23), channel_id=1, source_target_pairs={{0,8},{8,0},{1,9},{9,1},{2,10},{10,2},{3,11},{11,3},{4,12},{12,4},... | collective-permute-start | bytes 1572872 | tf_op jit(solution)/shard_map/ppermute | solution.py:282
  50.9 27.5 %all_to_all.32.got_ref = f32[64,1,384]{2,1,0:T(1,128)S(1)} all-to-all(f32[64,1,384]{2,1,0:T(1,128)S(1)} %get-tuple-element.28), channel_id=1, replica_groups=mesh['xlo'=2,'zh'=8,'zl'=2,'core'=2,'xhi'=2,'y'=4] {'xlo','zh','zl','core'}, dimensions={0} | all-to-all | bytes 196608 | tf_op jit(solution)/shard_map/all_to_all | solution.py:348
  78.4 0.7 shard_map.47
  79.1 3.9 %all-to-all-start.4 = ((f32[32,1,256]{2,1,0:T(1,128)}), f32[32,1,256]{2,1,0:T(1,128)S(1)}, u32[]{:S(2)}, u32[]{:S(2)}) async-start(f32[32,1,256]{2,1,0:T(1,128)} %get-tuple-element.30), calls=%async_computation.4 | async-start | bytes 65536 | tf_op jit(solution)/shard_map/all_to_all | solution.py:380
  83.0 0.0 collective-permute-done.1
  83.0 0.0 copy-start.3
  83.0 1.2 copy-done.3
  84.2 0.1 shard_map.45
  84.3 3.5 %collective-permute-start.2 = (bf16[8,2,32,256]{3,2,1,0:T(8,128)(2,1)S(1)}, bf16[8,2,32,256]{3,2,1,0:T(8,128)(2,1)S(1)}, u32[]{:S(2)}, u32[]{:S(2)}) collective-permute-start(bf16[8,2,32,256]{3,2,1,0:T(8,128)(2,1)S(1)} %get-tuple-element.25), channel_id=1, source_target_pairs={{0,256},{256,0},{1,257},{257,1},{2,258},{258,2},{3,259},{259,3},{4... | collective-permute-start | bytes 786440 | tf_op jit(solution)/shard_map/ppermute | solution.py:282
  87.8 8.1 %all-to-all-done.4.rows_ref = f32[32,1,256]{2,1,0:T(1,128)S(1)} async-done(((f32[32,1,256]{2,1,0:T(1,128)}), f32[32,1,256]{2,1,0:T(1,128)S(1)}, u32[]{:S(2)}, u32[]{:S(2)}) %all-to-all-start.4) | async-done | bytes 32800 | tf_op jit(solution)/shard_map/all_to_all | solution.py:380
  95.9 0.9 shard_map.48
  96.8 6.5 %all-to-all-start.5 = ((f32[16,40,256]{2,1,0:T(8,128)}), f32[16,40,256]{2,1,0:T(8,128)S(1)}, u32[]{:S(2)}, u32[]{:S(2)}) async-start(f32[16,40,256]{2,1,0:T(8,128)} %shard_map.48), calls=%async_computation.5 | async-start | bytes 1310720 | tf_op jit(solution)/shard_map/all_to_all | solution.py:391
  103.3 0.0 collective-permute-done.2.refs_2_
  103.3 0.1 shard_map.46
  103.4 2.5 %collective-permute-start.3 = (bf16[8,32,256]{2,1,0:T(8,128)(2,1)S(1)}, bf16[8,32,256]{2,1,0:T(8,128)(2,1)S(1)}, u32[]{:S(2)}, u32[]{:S(2)}) collective-permute-start(bf16[8,32,256]{2,1,0:T(8,128)(2,1)S(1)} %get-tuple-element.27), channel_id=1, source_target_pairs={{0,16},{16,0},{1,17},{17,1},{2,18},{18,2},{3,19},{19,3},{4,20},{20... | collective-permute-start | bytes 393224 | tf_op jit(solution)/shard_map/ppermute | solution.py:282
  105.9 4.3 %collective-permute-done.3 = bf16[8,32,256]{2,1,0:T(8,128)(2,1)S(1)} collective-permute-done((bf16[8,32,256]{2,1,0:T(8,128)(2,1)S(1)}, bf16[8,32,256]{2,1,0:T(8,128)(2,1)S(1)}, u32[]{:S(2)}, u32[]{:S(2)}) %collective-permute-start.3) | collective-permute-done | bytes 131104 | tf_op jit(solution)/shard_map/ppermute | solution.py:282
  110.2 0.7 add_convert_fusion
  110.9 3.5 %all-to-all-done.5.refs_0_ = f32[16,40,256]{2,1,0:T(8,128)S(1)} async-done(((f32[16,40,256]{2,1,0:T(8,128)}), f32[16,40,256]{2,1,0:T(8,128)S(1)}, u32[]{:S(2)}, u32[]{:S(2)}) %all-to-all-start.5) | async-done | bytes 655392 | tf_op jit(solution)/shard_map/all_to_all | solution.py:391
  114.4 3.6 %all-to-all-start.2 = ((bf16[8,32,256]{2,1,0:T(8,128)(2,1)}), bf16[8,32,256]{2,1,0:T(8,128)(2,1)S(1)}, u32[]{:S(2)}, u32[]{:S(2)}) async-start(bf16[8,32,256]{2,1,0:T(8,128)(2,1)} %add_convert_fusion), calls=%async_computation.2 | async-start | bytes 262144 | tf_op jit(solution)/shard_map/all_to_all | solution.py:405
  118.0 11.7 %shard_map.49 = (f32[256,256]{1,0:T(8,128)S(1)}, f32[256,256]{1,0:T(8,128)}, f32[64,256]{1,0:T(8,128)S(1)}, f32[64,128]{1,0:T(8,128)S(1)}) custom-call(f32[16,40,256]{2,1,0:T(8,128)S(1)} %all-to-all-done.5.refs_0_), custom_call_target="tpu_custom_call" | custom-call | flops 11000000512 | tf_op jit(solution)/shard_map/pallas_call | solution.py:268
  129.7 2.8 %all-to-all-done.2.refs_0_ = bf16[8,32,256]{2,1,0:T(8,128)(2,1)S(1)} async-done(((bf16[8,32,256]{2,1,0:T(8,128)(2,1)}), bf16[8,32,256]{2,1,0:T(8,128)(2,1)S(1)}, u32[]{:S(2)}, u32[]{:S(2)}) %all-to-all-start.2) | async-done | bytes 131104 | tf_op jit(solution)/shard_map/all_to_all | solution.py:405
  132.5 1.2 shard_map.50
  (6 shorter events, 0.1 us)
Async XLA Ops:
  0.6 1.2 copy-start
  4.2 34.4 %copy-start.1 = (bf16[512,2048]{1,0:T(8,128)(2,1)S(1)}, bf16[512,2048]{1,0:T(8,128)(2,1)}, u32[]{:S(2)}) copy-start(bf16[512,2048]{1,0:T(8,128)(2,1)} %frames_ref.3) | copy-start | bytes 6291460
  29.6 13.2 %collective-permute-start = (bf16[512,256]{1,0:T(8,128)(2,1)S(1)}, bf16[512,256]{1,0:T(8,128)(2,1)}, u32[]{:S(2)}, u32[]{:S(2)}) collective-permute-start(bf16[512,256]{1,0:T(8,128)(2,1)S(1)} %bitcast.13), channel_id=1, source_target_pairs={{8,16},{24,32},{40,48},{56,64},{72,80},{88,96},{104,112},{120,128}... | collective-permute-start | bytes 786440 | tf_op jit(solution)/shard_map/ppermute | solution.py:326
  48.0 1.0 copy-start.2
  49.0 33.9 %collective-permute-start.1 = (bf16[32,32,256]{2,1,0:T(8,128)(2,1)}, bf16[32,32,256]{2,1,0:T(8,128)(2,1)S(1)}, u32[]{:S(2)}, u32[]{:S(2)}) collective-permute-start(bf16[32,32,256]{2,1,0:T(8,128)(2,1)} %get-tuple-element.23), channel_id=1, source_target_pairs={{0,8},{8,0},{1,9},{9,1},{2,10},{10,2},{3,11},{11,3},{4,12},{12,4},... | collective-permute-start | bytes 1572872 | tf_op jit(solution)/shard_map/ppermute | solution.py:282
  79.1 16.8 %all-to-all-start.4 = ((f32[32,1,256]{2,1,0:T(1,128)}), f32[32,1,256]{2,1,0:T(1,128)S(1)}, u32[]{:S(2)}, u32[]{:S(2)}) async-start(f32[32,1,256]{2,1,0:T(1,128)} %get-tuple-element.30), calls=%async_computation.4 | async-start | bytes 65536 | tf_op jit(solution)/shard_map/all_to_all | solution.py:380
  83.0 1.2 copy-start.3
  84.3 19.0 %collective-permute-start.2 = (bf16[8,2,32,256]{3,2,1,0:T(8,128)(2,1)S(1)}, bf16[8,2,32,256]{3,2,1,0:T(8,128)(2,1)S(1)}, u32[]{:S(2)}, u32[]{:S(2)}) collective-permute-start(bf16[8,2,32,256]{3,2,1,0:T(8,128)(2,1)S(1)} %get-tuple-element.25), channel_id=1, source_target_pairs={{0,256},{256,0},{1,257},{257,1},{2,258},{258,2},{3,259},{259,3},{4... | collective-permute-start | bytes 786440 | tf_op jit(solution)/shard_map/ppermute | solution.py:282
  96.8 17.6 %all-to-all-start.5 = ((f32[16,40,256]{2,1,0:T(8,128)}), f32[16,40,256]{2,1,0:T(8,128)S(1)}, u32[]{:S(2)}, u32[]{:S(2)}) async-start(f32[16,40,256]{2,1,0:T(8,128)} %shard_map.48), calls=%async_computation.5 | async-start | bytes 1310720 | tf_op jit(solution)/shard_map/all_to_all | solution.py:391
  103.4 6.9 %collective-permute-start.3 = (bf16[8,32,256]{2,1,0:T(8,128)(2,1)S(1)}, bf16[8,32,256]{2,1,0:T(8,128)(2,1)S(1)}, u32[]{:S(2)}, u32[]{:S(2)}) collective-permute-start(bf16[8,32,256]{2,1,0:T(8,128)(2,1)S(1)} %get-tuple-element.27), channel_id=1, source_target_pairs={{0,16},{16,0},{1,17},{17,1},{2,18},{18,2},{3,19},{19,3},{4,20},{20... | collective-permute-start | bytes 393224 | tf_op jit(solution)/shard_map/ppermute | solution.py:282
  114.4 18.1 %all-to-all-start.2 = ((bf16[8,32,256]{2,1,0:T(8,128)(2,1)}), bf16[8,32,256]{2,1,0:T(8,128)(2,1)S(1)}, u32[]{:S(2)}, u32[]{:S(2)}) async-start(bf16[8,32,256]{2,1,0:T(8,128)(2,1)} %add_convert_fusion), calls=%async_computation.2 | async-start | bytes 262144 | tf_op jit(solution)/shard_map/all_to_all | solution.py:405

commit v4 on v3

--- a/solution.py
+++ b/solution.py
@@ -65,14 +65,25 @@
     diagonal = jnp.where(eye, a, 0.0)
     down = lax.rsqrt(jnp.sum(diagonal, axis=1, keepdims=True))
     along = lax.rsqrt(jnp.sum(diagonal, axis=0, keepdims=True))
-    s = jnp.concatenate([a * down * along, eye.astype(jnp.float32)], axis=1)
+    left, right = a * down * along, eye.astype(jnp.float32)
     rows = []
     for b in range(n // nb):
-        t = inverse_factor(s[:nb, nb * b : nb * b + nb])
-        p = dot(t, s[:nb])
-        rows.append(p[:, n:])
+        start = nb * b // 128 * 128
+        stop = min(n, -(-nb * (b + 1) // 128) * 128)
+        left = left[:, start - n :]
+        at = nb * b - start
+        t = inverse_factor(left[:nb, at : at + nb])
+        both = jnp.concatenate([left, right[:, :stop]], axis=1)
+        p = dot(t, both[:nb])
+        here = p[:, n - start :]
+        rows.append(here if stop == n else jnp.concatenate([here, right[:nb, stop:]], axis=1))
         if nb * (b + 1) < n:
-            s = s[nb:] - dot(p[:, nb * (b + 1) : n], p, ((0,), (0,)))
+            both = both[nb:] - dot(p[:, at + nb : n - start], p, ((0,), (0,)))
+            left = both[:, : n - start]
+            right_done, right_rest = both[:, n - start :], right[nb:]
+            right = right_done
+            if stop < n:
+                right = jnp.concatenate([right_done, right_rest[:, stop:]], axis=1)
     return jnp.concatenate(rows, axis=0) * along
 
 
@@ -249,7 +260,7 @@
         sums = sums.reshape(groups, 2, owned, vecs)
         low, high = sums[:, 0], sums[:, 1]
         part = slice(i * groups, (i + 1) * groups)
-        kept_ref[part] = jnp.where(core == 0, low, high)
+        kept_ref[part] = jnp.where(core == 0, low, high).astype(kept_ref.dtype)
         given_ref[part] = jnp.where(core == 0, high, low).astype(given_ref.dtype)
 
 
@@ -258,8 +269,8 @@
         return (slice(None),) * axis + (which,)
 
     own, other = at(place_ref[0]), at(1 - place_ref[0])
-    mine_ref[...] = kept_ref[own] + got_ref[own].astype(jnp.float32)
-    given_ref[...] = (kept_ref[other] + got_ref[other].astype(jnp.float32)).astype(given_ref.dtype)
+    mine_ref[...] = kept_ref[own].astype(jnp.float32) + got_ref[own].astype(jnp.float32)
+    given_ref[...] = (kept_ref[other].astype(jnp.float32) + got_ref[other].astype(jnp.float32)).astype(given_ref.dtype)
 
 
 def call(kernel, out_shape, *args, scalars=0, unread=0, scratch=(), flops=0):
@@ -358,7 +369,7 @@
     half = (2 * n_z, owned, vecs)
     kept, given = call(
         contract_kernel,
-        [jax.ShapeDtypeStruct(half, f32), jax.ShapeDtypeStruct(half, bf16)],
+        [jax.ShapeDtypeStruct(half, bf16), jax.ShapeDtypeStruct(half, bf16)],
         core[None],
         frames,
         on_chip,

time: 134 us -> 134 us (level)
  no operation moved by 1% of the time
where the time goes in v4:
time: 134 us; the launch traced here: 133 us
  blocking collectives  54.8 us (41%)
  starting transfers between devices  30.8 us (23%)
  Pallas kernels  20.7 us (15%)
  waiting for transfers between devices  19.3 us (14%)
  local copies, waits for them, and re-layouts  3.06 us (2%)
  matrix products  2.31 us (2%)
    all_to_all x1, blocking collectives, per_device(): got = lax.all_to_all(sent, TIME, 0, 0, tiled=True)  27.5 us
    pallas_call x10, Pallas kernels, call(): pl.pallas_call(kernel, out_shape=out_shape, in_specs=[scalar] * scalars +...  20.7 us
    all_to_all x1, blocking collectives, per_device(): packed = lax.all_to_all(packed, FEAT, 0, 0, tiled=True)  14 us
    all_to_all x1, blocking collectives, per_device(): lax.all_to_all(centred, FEAT, 0, 0, tiled=True).reshape(rows, vecs)  11.2 us
    ppermute x1, starting transfers between devices, per_device(): lax.ppermute(centred, TIME, pairs + [(b, a) for a, b in pairs])  9.01 us
    all_to_all x1, waiting for transfers between devices, per_device(): gram = lax.all_to_all(gram, ('zh', 'zl', 'core'), 0, 0, tiled=True)  8.26 us
    ppermute x3, starting transfers between devices, swap(): return lax.ppermute(x, axis, [(0, 1), (1, 0)])  7.94 us
    all_to_all x1, starting transfers between devices, per_device(): slices = lax.all_to_all(slices, ('xlo',) + FEAT, 0, 0, tiled=True)  6.47 us
  transfers between devices with their start and end apart: 7, of which 5 were waited for; matrix products, arithmetic and copies ran while one was open for 1% of the time, Pallas kernels for 11%

profile of v4, /device:TPU:6, one launch (start us, length us, event | category | flops | bytes accessed | tf_op | source)
XLA Modules:
  0.0 132.7 jit_solution(2851797326289707491)
XLA Ops:
  0.6 0.0 copy-start
  0.6 1.2 copy-done
  1.9 2.3 %fusion.6 = (f32[256]{0:T(256)S(1)}, f32[512,256]{1,0:T(8,128)S(1)}) fusion(bf16[512,2048]{1,0:T(8,128)(2,1)} %frames_ref.3, bf16[2048,256]{1,0:T(8,128)(2,1)S(1)} %copy-done), kind=kOutput, calls=%fused_computation.16 | convolution fusion | flops 537001728 | bytes 3671040 | tf_op jit(solution)/shard_map/dot_general | solution.py:14
  4.2 0.0 copy-start.1
  4.3 14.0 %all_to_all.30.got_ref = bf16[8,80,256]{2,1,0:T(8,128)(2,1)S(1)} all-to-all(bf16[8,80,256]{2,1,0:T(8,128)(2,1)S(1)} %pad_maximum_fusion), channel_id=1, replica_groups=mesh['xlo'=2,'zh'=8,'zl'=2,'core'=2,'xhi'=2,'y'=4] {'xhi','y'}, dimensions={0} | all-to-all | bytes 655360 | tf_op jit(solution)/shard_map/all_to_all | solution.py:325
  18.3 0.1 shard_map.41
  18.4 11.2 %all_to_all.31 = bf16[8,64,256]{2,1,0:T(8,128)(2,1)S(1)} all-to-all(bf16[8,64,256]{2,1,0:T(8,128)(2,1)S(1)} %get-tuple-element.19), channel_id=1, replica_groups=mesh['xlo'=2,'zh'=8,'zl'=2,'core'=2,'xhi'=2,'y'=4] {'xhi','y'}, dimensions={0} | all-to-all | bytes 524288 | tf_op jit(solution)/shard_map/all_to_all | solution.py:335
  29.6 9.0 %collective-permute-start = (bf16[512,256]{1,0:T(8,128)(2,1)S(1)}, bf16[512,256]{1,0:T(8,128)(2,1)}, u32[]{:S(2)}, u32[]{:S(2)}) collective-permute-start(bf16[512,256]{1,0:T(8,128)(2,1)S(1)} %bitcast.13), channel_id=1, source_target_pairs={{8,16},{24,32},{40,48},{56,64},{72,80},{88,96},{104,112},{120,128}... | collective-permute-start | bytes 786440 | tf_op jit(solution)/shard_map/ppermute | solution.py:337
  38.6 0.0 copy-done.1
  38.6 0.8 shard_map.42.shift_ref
  39.4 0.1 pad_add_fusion.place_ref
  39.5 2.2 %all_gather.3.first_ref = bf16[2,512,256]{2,1,0:T(8,128)(2,1)S(1)} all-gather(bf16[1,512,256]{2,1,0:T(8,128)(2,1)S(1)} %bitcast.14), channel_id=1, replica_groups=mesh['xlo'=2,'zh'=8,'zl'=2,'core'=2,'xhi'=2,'y'=4] {'core'}, dimensions={0}, use_global_device_ids=true | all-gather | bytes 786432 | tf_op jit(solution)/shard_map/all_gather | solution.py:338
  41.7 1.1 collective-permute-done.second_ref
  42.7 1.6 %shard_map.43 = (f32[64,1,384]{2,1,0:T(1,128)S(1)}, f32[8,256]{1,0:T(8,128)S(1)}) custom-call(s32[4]{0:T(128)S(1)} %pad_add_fusion.place_ref, bf16[512,256]{1,0:T(8,128)(2,1)S(1)} %bitcast.15, bf16[2,512,256]{2,1,0:T(8,128)(2,1)S(1)} %all_gather.3.first_ref, bf16[512,256]{1,0:T(8,128)(2,1)} %collective-permute-done.second_ref, ...), custom_call_target="tpu_custom_call" | custom-call | tf_op jit(solution)/shard_map/pallas_call | solution.py:279
  44.4 3.6 %shard_map.44 = (bf16[32,32,256]{2,1,0:T(8,128)(2,1)S(1)}, bf16[32,32,256]{2,1,0:T(8,128)(2,1)}) custom-call(s32[1]{0:T(128)} %bitcast.2.core_ref, bf16[512,2048]{1,0:T(8,128)(2,1)S(1)} %copy-done.1, bf16[2,512,256]{2,1,0:T(8,128)(2,1)S(1)} %all_gather.3.first_ref, bf16[512,256]{1,0:T(8,128)(2,1)} %collective-permute-done.second_ref, ...), custom_call_target="tpu_custom_call" | custom-call | flops 1073741824 | tf_op jit(solution)/shard_map/pallas_call | solution.py:279
  48.0 0.0 copy-start.2
  48.0 0.8 copy-done.2
  48.8 1.9 %collective-permute-start.1 = (bf16[32,32,256]{2,1,0:T(8,128)(2,1)}, bf16[32,32,256]{2,1,0:T(8,128)(2,1)S(1)}, u32[]{:S(2)}, u32[]{:S(2)}) collective-permute-start(bf16[32,32,256]{2,1,0:T(8,128)(2,1)} %get-tuple-element.23), channel_id=1, source_target_pairs={{0,8},{8,0},{1,9},{9,1},{2,10},{10,2},{3,11},{11,3},{4,12},{12,4},... | collective-permute-start | bytes 1572872 | tf_op jit(solution)/shard_map/ppermute | solution.py:293
  50.7 27.5 %all_to_all.32.got_ref = f32[64,1,384]{2,1,0:T(1,128)S(1)} all-to-all(f32[64,1,384]{2,1,0:T(1,128)S(1)} %get-tuple-element.28), channel_id=1, replica_groups=mesh['xlo'=2,'zh'=8,'zl'=2,'core'=2,'xhi'=2,'y'=4] {'xlo','zh','zl','core'}, dimensions={0} | all-to-all | bytes 196608 | tf_op jit(solution)/shard_map/all_to_all | solution.py:359
  78.2 0.7 shard_map.47
  78.9 3.9 %all-to-all-start.4 = ((f32[32,1,256]{2,1,0:T(1,128)}), f32[32,1,256]{2,1,0:T(1,128)S(1)}, u32[]{:S(2)}, u32[]{:S(2)}) async-start(f32[32,1,256]{2,1,0:T(1,128)} %get-tuple-element.30), calls=%async_computation.4 | async-start | bytes 65536 | tf_op jit(solution)/shard_map/all_to_all | solution.py:391
  82.8 0.0 collective-permute-done.1
  82.8 0.0 copy-start.3
  82.8 1.0 copy-done.3
  83.8 0.1 shard_map.45
  83.9 3.5 %collective-permute-start.2 = (bf16[8,2,32,256]{3,2,1,0:T(8,128)(2,1)S(1)}, bf16[8,2,32,256]{3,2,1,0:T(8,128)(2,1)S(1)}, u32[]{:S(2)}, u32[]{:S(2)}) collective-permute-start(bf16[8,2,32,256]{3,2,1,0:T(8,128)(2,1)S(1)} %get-tuple-element.25), channel_id=1, source_target_pairs={{0,256},{256,0},{1,257},{257,1},{2,258},{258,2},{3,259},{259,3},{4... | collective-permute-start | bytes 786440 | tf_op jit(solution)/shard_map/ppermute | solution.py:293
  87.5 8.3 %all-to-all-done.4.rows_ref = f32[32,1,256]{2,1,0:T(1,128)S(1)} async-done(((f32[32,1,256]{2,1,0:T(1,128)}), f32[32,1,256]{2,1,0:T(1,128)S(1)}, u32[]{:S(2)}, u32[]{:S(2)}) %all-to-all-start.4) | async-done | bytes 32800 | tf_op jit(solution)/shard_map/all_to_all | solution.py:391
  95.7 0.9 shard_map.48
  96.6 6.5 %all-to-all-start.5 = ((f32[16,40,256]{2,1,0:T(8,128)}), f32[16,40,256]{2,1,0:T(8,128)S(1)}, u32[]{:S(2)}, u32[]{:S(2)}) async-start(f32[16,40,256]{2,1,0:T(8,128)} %shard_map.48), calls=%async_computation.5 | async-start | bytes 1310720 | tf_op jit(solution)/shard_map/all_to_all | solution.py:402
  103.1 0.0 collective-permute-done.2.refs_2_
  103.1 0.1 shard_map.46
  103.2 2.5 %collective-permute-start.3 = (bf16[8,32,256]{2,1,0:T(8,128)(2,1)S(1)}, bf16[8,32,256]{2,1,0:T(8,128)(2,1)S(1)}, u32[]{:S(2)}, u32[]{:S(2)}) collective-permute-start(bf16[8,32,256]{2,1,0:T(8,128)(2,1)S(1)} %get-tuple-element.27), channel_id=1, source_target_pairs={{0,16},{16,0},{1,17},{17,1},{2,18},{18,2},{3,19},{19,3},{4,20},{20... | collective-permute-start | bytes 393224 | tf_op jit(solution)/shard_map/ppermute | solution.py:293
  105.7 4.3 %collective-permute-done.3 = bf16[8,32,256]{2,1,0:T(8,128)(2,1)S(1)} collective-permute-done((bf16[8,32,256]{2,1,0:T(8,128)(2,1)S(1)}, bf16[8,32,256]{2,1,0:T(8,128)(2,1)S(1)}, u32[]{:S(2)}, u32[]{:S(2)}) %collective-permute-start.3) | collective-permute-done | bytes 131104 | tf_op jit(solution)/shard_map/ppermute | solution.py:293
  110.0 0.7 add_convert_fusion
  110.7 3.5 %all-to-all-done.5.refs_0_ = f32[16,40,256]{2,1,0:T(8,128)S(1)} async-done(((f32[16,40,256]{2,1,0:T(8,128)}), f32[16,40,256]{2,1,0:T(8,128)S(1)}, u32[]{:S(2)}, u32[]{:S(2)}) %all-to-all-start.5) | async-done | bytes 655392 | tf_op jit(solution)/shard_map/all_to_all | solution.py:402
  114.2 3.6 %all-to-all-start.2 = ((bf16[8,32,256]{2,1,0:T(8,128)(2,1)}), bf16[8,32,256]{2,1,0:T(8,128)(2,1)S(1)}, u32[]{:S(2)}, u32[]{:S(2)}) async-start(bf16[8,32,256]{2,1,0:T(8,128)(2,1)} %add_convert_fusion), calls=%async_computation.2 | async-start | bytes 262144 | tf_op jit(solution)/shard_map/all_to_all | solution.py:416
  117.8 11.6 %shard_map.49 = (f32[256,256]{1,0:T(8,128)S(1)}, f32[256,256]{1,0:T(8,128)}, f32[64,256]{1,0:T(8,128)S(1)}, f32[64,128]{1,0:T(8,128)S(1)}) custom-call(f32[16,40,256]{2,1,0:T(8,128)S(1)} %all-to-all-done.5.refs_0_), custom_call_target="tpu_custom_call" | custom-call | flops 11000000512 | tf_op jit(solution)/shard_map/pallas_call | solution.py:279
  129.4 2.1 %all-to-all-done.2.refs_0_ = bf16[8,32,256]{2,1,0:T(8,128)(2,1)S(1)} async-done(((bf16[8,32,256]{2,1,0:T(8,128)(2,1)}), bf16[8,32,256]{2,1,0:T(8,128)(2,1)S(1)}, u32[]{:S(2)}, u32[]{:S(2)}) %all-to-all-start.2) | async-done | bytes 131104 | tf_op jit(solution)/shard_map/all_to_all | solution.py:416
  131.5 1.2 shard_map.50
  (6 shorter events, 0.1 us)
Async XLA Ops:
  0.6 1.2 copy-start
  4.2 34.4 %copy-start.1 = (bf16[512,2048]{1,0:T(8,128)(2,1)S(1)}, bf16[512,2048]{1,0:T(8,128)(2,1)}, u32[]{:S(2)}) copy-start(bf16[512,2048]{1,0:T(8,128)(2,1)} %frames_ref.3) | copy-start | bytes 6291460
  29.6 13.2 %collective-permute-start = (bf16[512,256]{1,0:T(8,128)(2,1)S(1)}, bf16[512,256]{1,0:T(8,128)(2,1)}, u32[]{:S(2)}, u32[]{:S(2)}) collective-permute-start(bf16[512,256]{1,0:T(8,128)(2,1)S(1)} %bitcast.13), channel_id=1, source_target_pairs={{8,16},{24,32},{40,48},{56,64},{72,80},{88,96},{104,112},{120,128}... | collective-permute-start | bytes 786440 | tf_op jit(solution)/shard_map/ppermute | solution.py:337
  48.0 0.8 copy-start.2
  48.8 33.9 %collective-permute-start.1 = (bf16[32,32,256]{2,1,0:T(8,128)(2,1)}, bf16[32,32,256]{2,1,0:T(8,128)(2,1)S(1)}, u32[]{:S(2)}, u32[]{:S(2)}) collective-permute-start(bf16[32,32,256]{2,1,0:T(8,128)(2,1)} %get-tuple-element.23), channel_id=1, source_target_pairs={{0,8},{8,0},{1,9},{9,1},{2,10},{10,2},{3,11},{11,3},{4,12},{12,4},... | collective-permute-start | bytes 1572872 | tf_op jit(solution)/shard_map/ppermute | solution.py:293
  78.9 16.8 %all-to-all-start.4 = ((f32[32,1,256]{2,1,0:T(1,128)}), f32[32,1,256]{2,1,0:T(1,128)S(1)}, u32[]{:S(2)}, u32[]{:S(2)}) async-start(f32[32,1,256]{2,1,0:T(1,128)} %get-tuple-element.30), calls=%async_computation.4 | async-start | bytes 65536 | tf_op jit(solution)/shard_map/all_to_all | solution.py:391
  82.8 1.0 copy-start.3
  83.9 19.2 %collective-permute-start.2 = (bf16[8,2,32,256]{3,2,1,0:T(8,128)(2,1)S(1)}, bf16[8,2,32,256]{3,2,1,0:T(8,128)(2,1)S(1)}, u32[]{:S(2)}, u32[]{:S(2)}) collective-permute-start(bf16[8,2,32,256]{3,2,1,0:T(8,128)(2,1)S(1)} %get-tuple-element.25), channel_id=1, source_target_pairs={{0,256},{256,0},{1,257},{257,1},{2,258},{258,2},{3,259},{259,3},{4... | collective-permute-start | bytes 786440 | tf_op jit(solution)/shard_map/ppermute | solution.py:293
  96.6 17.6 %all-to-all-start.5 = ((f32[16,40,256]{2,1,0:T(8,128)}), f32[16,40,256]{2,1,0:T(8,128)S(1)}, u32[]{:S(2)}, u32[]{:S(2)}) async-start(f32[16,40,256]{2,1,0:T(8,128)} %shard_map.48), calls=%async_computation.5 | async-start | bytes 1310720 | tf_op jit(solution)/shard_map/all_to_all | solution.py:402
  103.2 6.9 %collective-permute-start.3 = (bf16[8,32,256]{2,1,0:T(8,128)(2,1)S(1)}, bf16[8,32,256]{2,1,0:T(8,128)(2,1)S(1)}, u32[]{:S(2)}, u32[]{:S(2)}) collective-permute-start(bf16[8,32,256]{2,1,0:T(8,128)(2,1)S(1)} %get-tuple-element.27), channel_id=1, source_target_pairs={{0,16},{16,0},{1,17},{17,1},{2,18},{18,2},{3,19},{19,3},{4,20},{20... | collective-permute-start | bytes 393224 | tf_op jit(solution)/shard_map/ppermute | solution.py:293
  114.2 17.3 %all-to-all-start.2 = ((bf16[8,32,256]{2,1,0:T(8,128)(2,1)}), bf16[8,32,256]{2,1,0:T(8,128)(2,1)S(1)}, u32[]{:S(2)}, u32[]{:S(2)}) async-start(bf16[8,32,256]{2,1,0:T(8,128)(2,1)} %add_convert_fusion), calls=%async_computation.2 | async-start | bytes 262144 | tf_op jit(solution)/shard_map/all_to_all | solution.py:416
